TPU v7x, 32 devices: a whole 2x2x4 slice. The times are simulated.
32 devices in a mesh: dp: 8 (over z, y), section: 4 (over x, core).
Axes of the slice: x: 2, y: 2, z: 4, core: 2. Of those that a mesh axis runs over, the one named last changes fastest.
Arguments:
- tokens: bfloat16 [24, 512, 768], P('dp'), may hold values from -6 to 6
- lengths: int32 [24], P('dp'), may hold values from 64 to 512, as said below
- w_main: bfloat16 [4, 768, 3072], P('section'), may hold values from -2 to 2
- w_down_half: bfloat16 [4, 1536, 768], P('section'), may hold values from -0.21875 to 0.21875
- out_bias: float32 [4, 768], P('section'), may hold values from -3 to 3
- ln_gain: float32 [4, 768], P('section'), may hold values from 0.25 to 1.75
- ln_bias: float32 [4, 768], P('section'), may hold values from -3 to 3
- cotangent: bfloat16 [24, 512, 768], P('dp'), may hold values from -6 to 6
Outputs:
- section_out: bfloat16 [4, 24, 512, 768], P('section', 'dp')
- section_in_grad: bfloat16 [4, 24, 512, 768], P('section', 'dp')
- grad_w_main: float32 [4, 768, 3072], P('section')
- grad_w_down: float32 [4, 1536, 768], P('section')
- grad_out_bias: float32 [4, 768], P('section')
- grad_ln_gain: float32 [4, 768], P('section')
- grad_ln_bias: float32 [4, 768], P('section')
Inputs may be any that keep to these rules, and one draw needn't show every extreme that they name: `lengths`: one sequence has exactly 512 valid tokens and one exactly 64.
All inputs are finite; a program needn't handle non-finite values.
Results may differ from a plain program's by a relative error of at most 0.015.
Values may be sent and summed in bfloat16 or wider, within the bound.
A program may use at most 192 MiB of HBM per device.

v0:
```python
from functools import partial

import jax
import jax.numpy as jnp
from jax import lax
from jax.sharding import PartitionSpec as P

HEADS = 12
HEAD = 64


NORM_EPS = 1e-06
MASK_FILL = -1000000000.0
CONTRACT_ROWS = (((0,), (0,)), ((), ()))
CONTRACT_COLS = (((1,), (1,)), ((), ()))


def shortened(shard):

    def short(part):
        return part.astype(jnp.bfloat16) if part.dtype == jnp.float32 else part

    return jax.tree.map(short, shard)


def passed_along(block, axis, distance):
    devices = range(lax.axis_size(axis))
    route = [(i - distance, i) for i in devices if i - distance in devices]
    return lax.ppermute(block, axis, route)


def layer_stats(residual):
    center = jnp.mean(residual, axis=-1, keepdims=True)
    centred = residual - center
    spread = jnp.mean(centred * centred, axis=-1, keepdims=True)
    scale_row = lax.rsqrt(spread + NORM_EPS)
    return (centred * scale_row, scale_row)


def norm_back(grad_out, normed, scale_row, gain_row):
    weighted = grad_out * gain_row
    first_mean = jnp.mean(weighted, axis=-1, keepdims=True)
    second_mean = jnp.mean(weighted * normed, axis=-1, keepdims=True)
    return scale_row * (weighted - first_mean - normed * second_mean)


def send_back(grad_rows):
    return jax.tree.map(
        lambda part, own: part.astype(own.dtype),
        passed_along(shortened(grad_rows), "section", -1),
        grad_rows,
    )


def attention_parts(inputs, weights, bias_row, key_valid):
    seq_len, model_width = inputs.shape
    mixed_qkv = jnp.dot(
        inputs, weights[:, : 3 * model_width], preferred_element_type=jnp.float32
    ).astype(jnp.bfloat16)
    query_heads = mixed_qkv[:, :model_width].reshape(seq_len, HEADS, HEAD)
    key_heads = mixed_qkv[:, model_width : 2 * model_width].reshape(seq_len, HEADS, HEAD)
    value_heads = mixed_qkv[:, 2 * model_width :].reshape(seq_len, HEADS, HEAD)
    scores = jnp.einsum(
        "qhd,khd->hqk", query_heads, key_heads, preferred_element_type=jnp.float32
    ) * HEAD ** (-0.5)
    scores = jnp.where(key_valid[None, None, :], scores, MASK_FILL)
    soft_full = jax.nn.softmax(scores, axis=-1)
    soft_low = soft_full.astype(jnp.bfloat16)
    context = jnp.einsum("hqk,khd->qhd", soft_low, value_heads, preferred_element_type=jnp.float32)
    context = context.reshape(seq_len, model_width).astype(jnp.bfloat16)
    residual = inputs.astype(jnp.float32) + (
        jnp.dot(context, weights[:, 3 * model_width :], preferred_element_type=jnp.float32)
        + bias_row
    )
    normed, scale_row = layer_stats(residual)
    return (query_heads, key_heads, value_heads, soft_full, soft_low, context, normed, scale_row)


def feed_parts(inputs, weights, down_full, bias_row):
    pre_act = jnp.dot(inputs, weights, preferred_element_type=jnp.float32)
    hidden = jax.nn.gelu(pre_act, approximate=False).astype(jnp.bfloat16)
    residual = inputs.astype(jnp.float32) + (
        jnp.dot(hidden, down_full, preferred_element_type=jnp.float32) + bias_row
    )
    normed, scale_row = layer_stats(residual)
    return (pre_act, hidden, normed, scale_row)


def keep_slot(stored, entry, held_slot, is_live):
    previous = lax.dynamic_index_in_dim(stored, held_slot, 0, keepdims=False)
    return lax.dynamic_update_index_in_dim(
        stored, jnp.where(is_live, entry, previous), held_slot, 0
    )


def on_device(tokens, lengths, w_main, w_down_half, out_bias, ln_gain, ln_bias, cotangent):
    section_index = lax.axis_index("section")
    section_count = lax.axis_size("section")
    seq_count, seq_len, model_width = tokens.shape
    weights = w_main[0]
    wide_width = weights.shape[1]
    bias_row = out_bias[0]
    gain_row = ln_gain[0]
    shift_row = ln_bias[0]
    partner_rows = passed_along(w_down_half, "section", 1)
    down_full = jnp.concatenate([partner_rows[0], w_down_half[0]], axis=0)
    positions = lax.iota(jnp.int32, seq_len)
    branch_kind = 1 + section_index % 2

    def attend_forward(inputs, length):
        parts = attention_parts(inputs, weights, bias_row, positions < length)
        return (parts[6] * gain_row + shift_row).astype(jnp.bfloat16)

    def feed_forward(inputs, length):
        parts = feed_parts(inputs, weights, down_full, bias_row)
        return (parts[2] * gain_row + shift_row).astype(jnp.bfloat16)

    def spare_forward(inputs, length):
        return jnp.zeros_like(inputs)

    def norm_grads(seed_grad, normed, scale_row):
        grad_out = seed_grad.astype(jnp.float32)
        grad_gain = jnp.sum(grad_out * normed, axis=0)
        grad_shift = jnp.sum(grad_out, axis=0)
        grad_resid = norm_back(grad_out, normed, scale_row, gain_row)
        return (grad_resid, jnp.sum(grad_resid, axis=0), grad_gain, grad_shift)

    def attend_input(inputs, length, seed_grad):
        query_heads, key_heads, value_heads, soft_full, soft_low, context, normed, scale_row = (
            attention_parts(inputs, weights, bias_row, positions < length)
        )
        grad_resid, grad_bias, grad_gain, grad_shift = norm_grads(seed_grad, normed, scale_row)
        grad_branch = grad_resid.astype(jnp.bfloat16)
        out_weight = weights[:, 3 * model_width :]
        grad_context = lax.dot_general(
            grad_branch, out_weight, CONTRACT_COLS, preferred_element_type=jnp.float32
        )
        grad_context = grad_context.astype(jnp.bfloat16).reshape(seq_len, HEADS, HEAD)
        grad_values = jnp.einsum(
            "hqk,qhd->khd", soft_low, grad_context, preferred_element_type=jnp.float32
        )
        grad_probs = jnp.einsum(
            "qhd,khd->hqk", grad_context, value_heads, preferred_element_type=jnp.float32
        )
        grad_scores = soft_full * (
            grad_probs - jnp.sum(soft_full * grad_probs, axis=-1, keepdims=True)
        )
        grad_scores = grad_scores.astype(jnp.bfloat16) * HEAD ** (-0.5)
        grad_query = jnp.einsum(
            "hqk,khd->qhd", grad_scores, key_heads, preferred_element_type=jnp.float32
        )
        grad_keys = jnp.einsum(
            "hqk,qhd->khd", grad_scores, query_heads, preferred_element_type=jnp.float32
        )
        grad_qkv = jnp.concatenate(
            [
                grad_query.reshape(seq_len, model_width),
                grad_keys.reshape(seq_len, model_width),
                grad_values.reshape(seq_len, model_width),
            ],
            axis=1,
        ).astype(jnp.bfloat16)
        grad_inputs = grad_resid + lax.dot_general(
            grad_qkv,
            weights[:, : 3 * model_width],
            CONTRACT_COLS,
            preferred_element_type=jnp.float32,
        )
        left_wide = jnp.pad(context, ((0, 0), (0, wide_width - model_width)))
        grad_wide = jnp.pad(grad_qkv, ((0, 0), (0, wide_width - 3 * model_width)))
        return (
            grad_inputs.astype(jnp.bfloat16),
            left_wide,
            grad_wide,
            grad_branch,
            grad_bias,
            grad_gain,
            grad_shift,
        )

    def feed_input(inputs, length, seed_grad):
        pre_act, hidden, normed, scale_row = feed_parts(inputs, weights, down_full, bias_row)
        grad_resid, grad_bias, grad_gain, grad_shift = norm_grads(seed_grad, normed, scale_row)
        grad_branch = grad_resid.astype(jnp.bfloat16)
        grad_hidden = lax.dot_general(
            grad_branch, down_full, CONTRACT_COLS, preferred_element_type=jnp.float32
        )
        gelu_value, gelu_pull = jax.vjp(partial(jax.nn.gelu, approximate=False), pre_act)
        grad_pre = gelu_pull(grad_hidden)[0].astype(jnp.bfloat16)
        grad_inputs = grad_resid + lax.dot_general(
            grad_pre, weights, CONTRACT_COLS, preferred_element_type=jnp.float32
        )
        return (
            grad_inputs.astype(jnp.bfloat16),
            hidden,
            grad_pre,
            grad_branch,
            grad_bias,
            grad_gain,
            grad_shift,
        )

    def spare_input(inputs, length, seed_grad):
        zero_row = jnp.zeros((model_width,), jnp.float32)
        zero_wide = jnp.zeros((seq_len, wide_width), jnp.bfloat16)
        return (
            jnp.zeros_like(inputs),
            zero_wide,
            zero_wide,
            jnp.zeros_like(inputs),
            zero_row,
            zero_row,
            zero_row,
        )

    def attend_weights(inputs, left_wide, grad_wide, grad_branch):
        grad_in_weight = lax.dot_general(
            inputs,
            grad_wide[:, : 3 * model_width],
            CONTRACT_ROWS,
            preferred_element_type=jnp.float32,
        )
        grad_out_weight = lax.dot_general(
            left_wide[:, :model_width],
            grad_branch,
            CONTRACT_ROWS,
            preferred_element_type=jnp.float32,
        )
        return (
            jnp.concatenate([grad_in_weight, grad_out_weight], axis=1),
            jnp.zeros(down_full.shape, jnp.float32),
        )

    def feed_weights(inputs, left_wide, grad_wide, grad_branch):
        grad_main_term = lax.dot_general(
            inputs, grad_wide, CONTRACT_ROWS, preferred_element_type=jnp.float32
        )
        grad_down_term = lax.dot_general(
            left_wide, grad_branch, CONTRACT_ROWS, preferred_element_type=jnp.float32
        )
        return (grad_main_term, grad_down_term)

    def spare_weights(inputs, left_wide, grad_wide, grad_branch):
        return (jnp.zeros(weights.shape, jnp.float32), jnp.zeros(down_full.shape, jnp.float32))

    input_kinds = [spare_input, attend_input, feed_input]
    weight_kinds = [spare_weights, attend_weights, feed_weights]
    steps_total = seq_count + section_count - 1
    blank_store = jnp.zeros_like(tokens)
    blank_rows = jnp.zeros((seq_len, model_width), jnp.bfloat16)

    def forward_step(time_step, carried):
        received, kept_in, kept_out = carried
        micro_index = time_step - section_index
        is_live = (micro_index >= 0) & (micro_index < seq_count)
        held_slot = jnp.clip(micro_index, 0, seq_count - 1)
        fresh_rows = lax.dynamic_index_in_dim(tokens, held_slot, 0, keepdims=False)
        inputs = jnp.where(section_index == 0, fresh_rows, received)
        length = lax.dynamic_index_in_dim(lengths, held_slot, 0, keepdims=False)
        result = lax.switch(
            jnp.where(is_live, branch_kind, 0),
            [spare_forward, attend_forward, feed_forward],
            inputs,
            length,
        )
        kept_in = keep_slot(kept_in, inputs, held_slot, is_live)
        kept_out = keep_slot(kept_out, result, held_slot, is_live)
        received = jax.tree.map(
            lambda part, own: part.astype(own.dtype),
            passed_along(shortened(result), "section", 1),
            result,
        )
        return (received, kept_in, kept_out)

    unused_rows, kept_in, kept_out = lax.fori_loop(
        0, steps_total, forward_step, (blank_rows, blank_store, blank_store)
    )
    zero_totals = (
        jnp.zeros(weights.shape, jnp.float32),
        jnp.zeros(down_full.shape, jnp.float32),
        jnp.zeros((model_width,), jnp.float32),
        jnp.zeros((model_width,), jnp.float32),
        jnp.zeros((model_width,), jnp.float32),
    )

    def input_part(time_step, received):
        micro_index = time_step - (section_count - 1 - section_index)
        is_live = (micro_index >= 0) & (micro_index < seq_count)
        held_slot = jnp.clip(micro_index, 0, seq_count - 1)
        outer_grad = lax.dynamic_index_in_dim(cotangent, held_slot, 0, keepdims=False)
        seed_grad = jnp.where(section_index == section_count - 1, outer_grad, received)
        inputs = lax.dynamic_index_in_dim(kept_in, held_slot, 0, keepdims=False)
        length = lax.dynamic_index_in_dim(lengths, held_slot, 0, keepdims=False)
        final_result = lax.switch(
            jnp.where(is_live, branch_kind, 0), input_kinds, inputs, length, seed_grad
        )
        return (is_live, held_slot, inputs, final_result)

    def backward_step(time_step, carried):
        received, kept_grad, accumulated_sums = carried
        is_live, held_slot, inputs, final_result = input_part(time_step, received)
        primary_term, down_projection_term = lax.switch(
            jnp.where(is_live, branch_kind, 0),
            weight_kinds,
            inputs,
            final_result[1],
            final_result[2],
            final_result[3],
        )
        summand_list = (primary_term, down_projection_term) + tuple(final_result[4:])
        accumulated_sums = tuple(
            (
                running_total + summand_value
                for running_total, summand_value in zip(accumulated_sums, summand_list)
            )
        )
        kept_grad = keep_slot(kept_grad, final_result[0], held_slot, is_live)
        received = send_back(final_result[0])
        return (received, kept_grad, accumulated_sums)

    unused_grad, kept_grad, accumulated_sums = lax.fori_loop(
        0, steps_total, backward_step, (blank_rows, blank_store, zero_totals)
    )
    grad_main, grad_down, grad_bias, grad_gain, grad_shift = accumulated_sums
    half_rows = down_full.shape[0] // 2
    attention_side = section_index % 2 == 0
    grad_main, grad_down, grad_bias, grad_gain, grad_shift = lax.psum(
        (grad_main, grad_down, grad_bias, grad_gain, grad_shift), "dp"
    )
    moved_rows = passed_along(grad_down[:half_rows].astype(jnp.bfloat16), "section", -1).astype(
        jnp.float32
    )
    grad_half = jnp.where(attention_side, moved_rows, grad_down[half_rows:])
    return (
        kept_out[None],
        kept_grad[None],
        grad_main[None],
        grad_half[None],
        grad_bias[None],
        grad_gain[None],
        grad_shift[None],
    )


def solution(mesh):
    in_specs = (
        P("dp", None, None),
        P("dp"),
        P("section", None, None),
        P("section", None, None),
        P("section", None),
        P("section", None),
        P("section", None),
        P("dp", None, None),
    )
    out_specs = (
        P("section", "dp", None, None),
        P("section", "dp", None, None),
        P("section", None, None),
        P("section", None, None),
        P("section", None),
        P("section", None),
        P("section", None),
    )
    return jax.shard_map(
        on_device, mesh=mesh, in_specs=in_specs, out_specs=out_specs, check_vma=False
    )
```

profile of v0, /device:TPU:4, one launch (start us, length us, event | category | flops | bytes accessed | tf_op | source)
XLA Modules:
  0.0 1610.3 jit_solution(8329672012258540977)
XLA Ops:
  20.7 203.6 %while.47 = (s32[]{:T(128)}, bf16[512,768]{1,0:T(8,128)(2,1)S(1)}, bf16[3,512,768]{2,1,0:T(8,128)(2,1)}, bf16[3,512,768]{2,1,0:T(8,128)(2,1)}, s32[]{:T(128)}, /...) while((s32[]{:T(128)}, bf16[512,768]{1,0:T(8,128)(2,1)S(1)}, ...), condition=%wide.region_10.11_spmd.clone, body=%wide.region_0.10_spmd.clone.sunk | while | flops 4939973120 | bytes 71667704 | solution.py:275
  24.3 22.6 %conditional.9 = (bf16[512,768]{1,0:T(8,128)(2,1)S(1)}) conditional(s32[]{:T(128)} %clamp.22, () %tuple.150, (bf16[512,768]{1,0:T(8,128)(2,1)S(1)}, bf16[768,3072]{1,0:T(8,128)(2,1)}, s32[3]{0:T(128)S(1)}, s32[]{:T(128)}, s32[512]{0:T(512)S(1)}, /*index=5*/f32[1,768]{1,0:T(1,128)S(1)}, f32[1,768]{1,0:T(1,128)S(1)}, ...), branch_computations={%region_1.1_spmd, %region_2.6_spmd, %region_7.9_spmd} | conditional | flops 4938793472 | bytes 59080796 | solution.py:260
  55.7 22.6 %conditional.9 = (bf16[512,768]{1,0:T(8,128)(2,1)S(1)}) conditional(s32[]{:T(128)} %clamp.22, () %tuple.150, (bf16[512,768]{1,0:T(8,128)(2,1)S(1)}, bf16[768,3072]{1,0:T(8,128)(2,1)}, s32[3]{0:T(128)S(1)}, s32[]{:T(128)}, s32[512]{0:T(512)S(1)}, /*index=5*/f32[1,768]{1,0:T(1,128)S(1)}, f32[1,768]{1,0:T(1,128)S(1)}, ...), branch_computations={%region_1.1_spmd, %region_2.6_spmd, %region_7.9_spmd} | conditional | flops 4938793472 | bytes 59080796 | solution.py:260
  78.3 10.8 collective-permute-start
  95.0 22.6 %conditional.9 = (bf16[512,768]{1,0:T(8,128)(2,1)S(1)}) conditional(s32[]{:T(128)} %clamp.22, () %tuple.150, (bf16[512,768]{1,0:T(8,128)(2,1)S(1)}, bf16[768,3072]{1,0:T(8,128)(2,1)}, s32[3]{0:T(128)S(1)}, s32[]{:T(128)}, s32[512]{0:T(512)S(1)}, /*index=5*/f32[1,768]{1,0:T(1,128)S(1)}, f32[1,768]{1,0:T(1,128)S(1)}, ...), branch_computations={%region_1.1_spmd, %region_2.6_spmd, %region_7.9_spmd} | conditional | flops 4938793472 | bytes 59080796 | solution.py:260
  117.6 8.5 collective-permute-start
  132.0 33.6 %collective-permute-start = (bf16[512,768]{1,0:T(8,128)(2,1)S(1)}, bf16[512,768]{1,0:T(8,128)(2,1)S(1)}, u32[]{:S(2)}, u32[]{:S(2)}) collective-permute-start(bf16[512,768]{1,0:T(8,128)(2,1)S(1)} %get-tuple-element.1431), channel_id=1, source_target_pairs={{0,1},{1,2},{2,3},{4,5},{5,6},{6,7},{8,9},{9,10},{10,11},{12,13},{... | collective-permute-start | bytes 2359304 | tf_op jit(solution)/shard_map/while/body/eval_jaxpr/ppermute | solution.py:29
  171.4 11.2 collective-permute-start
  188.5 33.6 %collective-permute-start = (bf16[512,768]{1,0:T(8,128)(2,1)S(1)}, bf16[512,768]{1,0:T(8,128)(2,1)S(1)}, u32[]{:S(2)}, u32[]{:S(2)}) collective-permute-start(bf16[512,768]{1,0:T(8,128)(2,1)S(1)} %get-tuple-element.1431), channel_id=1, source_target_pairs={{0,1},{1,2},{2,3},{4,5},{5,6},{6,7},{8,9},{9,10},{10,11},{12,13},{... | collective-permute-start | bytes 2359304 | tf_op jit(solution)/shard_map/while/body/eval_jaxpr/ppermute | solution.py:29
  225.9 774.0 %while.48 = (s32[]{:T(128)}, bf16[512,768]{1,0:T(8,128)(2,1)S(1)}, bf16[3,512,768]{2,1,0:T(8,128)(2,1)}, f32[768,3072]{1,0:T(8,128)}, f32[3072,768]{1,0:T(8,128)...) while((s32[]{:T(128)}, bf16[512,768]{1,0:T(8,128)(2,1)S(1)}, ...), condition=%wide.region_35.36_spmd.clone, body=%wide.region_11.35_spmd.clone.sunk | while | flops 14641400832 | bytes 312514048 | solution.py:321
  237.4 13.0 conditional.10
  251.6 9.2 conditional.11
  260.9 10.4 select_add_fusion.9
  271.4 8.5 select_add_fusion.10
  292.2 9.1 conditional.11
  301.3 13.1 select_add_fusion.9
  314.4 11.1 select_add_fusion.10
  338.0 9.1 conditional.11
  347.1 13.1 select_add_fusion.9
  360.2 11.1 select_add_fusion.10
  373.7 118.3 %collective-permute-done.1 = bf16[512,768]{1,0:T(8,128)(2,1)S(1)} collective-permute-done((bf16[512,768]{1,0:T(8,128)(2,1)}, bf16[512,768]{1,0:T(8,128)(2,1)S(1)}, u32[]{:S(2)}, u32[]{:S(2)}) %collective-permute-start.1) | collective-permute-done | bytes 786464 | tf_op jit(solution)/shard_map/while/body/eval_jaxpr/ppermute | solution.py:29
  494.6 114.1 %conditional.10 = (bf16[512,768]{1,0:T(8,128)(2,1)}, bf16[512,3072]{1,0:T(8,128)(2,1)}, bf16[512,3072]{1,0:T(8,128)(2,1)}, bf16[512,768]{1,0:T(8,128)(2,1)}, f32...) conditional(s32[]{:T(128)} %clamp.23, () %tuple.155, ...), branch_computations={%region_12.12_spmd, %region_13.23_spmd, %region_24.31_spmd} | conditional | flops 9799333888 | bytes 202308896 | solution.py:294
  504.8 11.2 fusion.154
  551.9 18.5 %fusion.110 = bf16[12,64,512]{2,1,0:T(8,128)(2,1)} fusion(bf16[512,12,64]{0,2,1:T(8,128)(2,1)} %bitcast.116, f32[12,512,512]{1,2,0:T(8,128)} %fusion.161, f32[12,512,512]{1,2,0:T(8,128)} %get-tuple-element.1043, f32[12,512]{1,0:T(8,128)S(1)} %get-tuple-element.1042), kind=kOutput, calls=%fused_computation.135 | convolution fusion | flops 434510336 | bytes 26763264 | tf_op jit(solution)/shard_map/while/body/eval_jaxpr/cond/branch_1_fun/hqk,khd->qhd/dot_general | solution.py:149
  570.4 18.7 %fusion.115 = bf16[12,64,512]{2,1,0:T(8,128)(2,1)} fusion(bf16[512,12,64]{0,2,1:T(8,128)(2,1)} %bitcast.118, f32[12,512,512]{1,2,0:T(8,128)} %fusion.161, f32[12,512,512]{1,2,0:T(8,128)} %get-tuple-element.1043, f32[12,512]{1,0:T(8,128)S(1)} %get-tuple-element.1042), kind=kOutput, calls=%fused_computation.136 | convolution fusion | flops 434510336 | bytes 26763264 | tf_op jit(solution)/shard_map/while/body/eval_jaxpr/cond/branch_1_fun/hqk,qhd->khd/dot_general | solution.py:152
  610.0 21.2 %conditional.11 = (f32[768,3072]{1,0:T(8,128)}, f32[3072,768]{1,0:T(8,128)}) conditional(s32[]{:T(128)} %clamp.23, () %tuple.158, (bf16[512,3072]{1,0:T(8,128)(2,1)}, bf16[512,768]{1,0:T(8,128)(2,1)S(1)}, bf16[512,3072]{1,0:T(8,128)(2,1)}, bf16[512,768]{1,0:T(8,128)(2,1)}) %tuple.159, (bf16[512,768]{1,0:T(8,128)(2,1)S(1)}, ...), branch_computations={%region_32.32_spmd, %region_33.33_spmd, %region_34.34_spmd} | conditional | flops 4831838208 | bytes 42467348 | solution.py:302
  618.7 8.0 pad_maximum_fusion
  631.2 13.1 select_add_fusion.9
  644.3 11.1 select_add_fusion.10
  666.6 113.9 %conditional.10 = (bf16[512,768]{1,0:T(8,128)(2,1)}, bf16[512,3072]{1,0:T(8,128)(2,1)}, bf16[512,3072]{1,0:T(8,128)(2,1)}, bf16[512,768]{1,0:T(8,128)(2,1)}, f32...) conditional(s32[]{:T(128)} %clamp.23, () %tuple.155, ...), branch_computations={%region_12.12_spmd, %region_13.23_spmd, %region_24.31_spmd} | conditional | flops 9799333888 | bytes 202308896 | solution.py:294
  676.8 11.2 fusion.154
  704.9 8.1 fusion.107
  724.0 18.5 %fusion.110 = bf16[12,64,512]{2,1,0:T(8,128)(2,1)} fusion(bf16[512,12,64]{0,2,1:T(8,128)(2,1)} %bitcast.116, f32[12,512,512]{1,2,0:T(8,128)} %fusion.161, f32[12,512,512]{1,2,0:T(8,128)} %get-tuple-element.1043, f32[12,512]{1,0:T(8,128)S(1)} %get-tuple-element.1042), kind=kOutput, calls=%fused_computation.135 | convolution fusion | flops 434510336 | bytes 26763264 | tf_op jit(solution)/shard_map/while/body/eval_jaxpr/cond/branch_1_fun/hqk,khd->qhd/dot_general | solution.py:149
  742.5 18.7 %fusion.115 = bf16[12,64,512]{2,1,0:T(8,128)(2,1)} fusion(bf16[512,12,64]{0,2,1:T(8,128)(2,1)} %bitcast.118, f32[12,512,512]{1,2,0:T(8,128)} %fusion.161, f32[12,512,512]{1,2,0:T(8,128)} %get-tuple-element.1043, f32[12,512]{1,0:T(8,128)S(1)} %get-tuple-element.1042), kind=kOutput, calls=%fused_computation.136 | convolution fusion | flops 434510336 | bytes 26763264 | tf_op jit(solution)/shard_map/while/body/eval_jaxpr/cond/branch_1_fun/hqk,qhd->khd/dot_general | solution.py:152
  781.8 21.4 %conditional.11 = (f32[768,3072]{1,0:T(8,128)}, f32[3072,768]{1,0:T(8,128)}) conditional(s32[]{:T(128)} %clamp.23, () %tuple.158, (bf16[512,3072]{1,0:T(8,128)(2,1)}, bf16[512,768]{1,0:T(8,128)(2,1)S(1)}, bf16[512,3072]{1,0:T(8,128)(2,1)}, bf16[512,768]{1,0:T(8,128)(2,1)}) %tuple.159, (bf16[512,768]{1,0:T(8,128)(2,1)S(1)}, ...), branch_computations={%region_32.32_spmd, %region_33.33_spmd, %region_34.34_spmd} | conditional | flops 4831838208 | bytes 42467348 | solution.py:302
  790.6 8.0 pad_maximum_fusion
  803.2 13.1 select_add_fusion.9
  816.4 11.1 select_add_fusion.10
  834.0 113.9 %conditional.10 = (bf16[512,768]{1,0:T(8,128)(2,1)}, bf16[512,3072]{1,0:T(8,128)(2,1)}, bf16[512,3072]{1,0:T(8,128)(2,1)}, bf16[512,768]{1,0:T(8,128)(2,1)}, f32...) conditional(s32[]{:T(128)} %clamp.23, () %tuple.155, ...), branch_computations={%region_12.12_spmd, %region_13.23_spmd, %region_24.31_spmd} | conditional | flops 9799333888 | bytes 202308896 | solution.py:294
  844.2 11.2 fusion.154
  891.1 18.5 %fusion.110 = bf16[12,64,512]{2,1,0:T(8,128)(2,1)} fusion(bf16[512,12,64]{0,2,1:T(8,128)(2,1)} %bitcast.116, f32[12,512,512]{1,2,0:T(8,128)} %fusion.161, f32[12,512,512]{1,2,0:T(8,128)} %get-tuple-element.1043, f32[12,512]{1,0:T(8,128)S(1)} %get-tuple-element.1042), kind=kOutput, calls=%fused_computation.135 | convolution fusion | flops 434510336 | bytes 26763264 | tf_op jit(solution)/shard_map/while/body/eval_jaxpr/cond/branch_1_fun/hqk,khd->qhd/dot_general | solution.py:149
  909.7 18.7 %fusion.115 = bf16[12,64,512]{2,1,0:T(8,128)(2,1)} fusion(bf16[512,12,64]{0,2,1:T(8,128)(2,1)} %bitcast.118, f32[12,512,512]{1,2,0:T(8,128)} %fusion.161, f32[12,512,512]{1,2,0:T(8,128)} %get-tuple-element.1043, f32[12,512]{1,0:T(8,128)S(1)} %get-tuple-element.1042), kind=kOutput, calls=%fused_computation.136 | convolution fusion | flops 434510336 | bytes 26763264 | tf_op jit(solution)/shard_map/while/body/eval_jaxpr/cond/branch_1_fun/hqk,qhd->khd/dot_general | solution.py:152
  949.2 21.2 %conditional.11 = (f32[768,3072]{1,0:T(8,128)}, f32[3072,768]{1,0:T(8,128)}) conditional(s32[]{:T(128)} %clamp.23, () %tuple.158, (bf16[512,3072]{1,0:T(8,128)(2,1)}, bf16[512,768]{1,0:T(8,128)(2,1)S(1)}, bf16[512,3072]{1,0:T(8,128)(2,1)}, bf16[512,768]{1,0:T(8,128)(2,1)}) %tuple.159, (bf16[512,768]{1,0:T(8,128)(2,1)S(1)}, ...), branch_computations={%region_32.32_spmd, %region_33.33_spmd, %region_34.34_spmd} | conditional | flops 4831838208 | bytes 42467348 | solution.py:302
  957.9 8.0 pad_maximum_fusion
  970.4 13.1 select_add_fusion.9
  983.5 11.1 select_add_fusion.10
  1000.0 569.1 %all-reduce.6.cloned.1.call-done = (f32[1,768,3072]{2,1,0:T(8,128)}, f32[3072,768]{1,0:T(8,128)}) async-done(((f32[1,768,3072]{2,1,0:T(8,128)}, f32[3072,768]{1,0:T(8,128)}), (f32[1,768,3072]{2,1,0:T(8,128)}, f32[3072,768]{1,0:T(8,128)})) %all-reduce.6.cloned.1.call-update) | async-done | bytes 18874384 | tf_op jit(solution)/shard_map/psum | solution.py:327
  1573.1 18.7 %all-reduce.2 = (f32[1,768]{1,0:T(1,128)}, f32[1,768]{1,0:T(1,128)}, f32[1,768]{1,0:T(1,128)}) all-reduce(f32[1,768]{1,0:T(1,128)S(1)} %broadcast_in_dim.94, f32[1,768]{1,0:T(1,128)S(1)} %broadcast_in_dim.95, f32[1,768]{1,0:T(1,128)S(1)} %broadcast_in_dim.96), channel_id=1, replica_groups=mesh['dp'=8,'section'=4] {'dp'}, use_global_device_ids=true, to_apply=%region_38.39 | all-reduce | flops 2304 | bytes 18432 | tf_op jit(solution)/shard_map/psum | solution.py:327
  (439 shorter events, 444.1 us)
Async XLA Ops:
  7.2 1562.0 %all-reduce.6.cloned.1.call-start = ((), (), s32[]{:S(2)}) async-start(), calls=%async_computation | async-start | bytes 37748736 | tf_op jit(solution)/shard_map/psum | solution.py:327
  7.2 6.1 collective-permute-start.2
  46.9 5.2 collective-permute-start
  78.3 13.1 collective-permute-start
  117.6 10.8 collective-permute-start
  132.0 35.8 %collective-permute-start = (bf16[512,768]{1,0:T(8,128)(2,1)S(1)}, bf16[512,768]{1,0:T(8,128)(2,1)S(1)}, u32[]{:S(2)}, u32[]{:S(2)}) collective-permute-start(bf16[512,768]{1,0:T(8,128)(2,1)S(1)} %get-tuple-element.1431), channel_id=1, source_target_pairs={{0,1},{1,2},{2,3},{4,5},{5,6},{6,7},{8,9},{9,10},{10,11},{12,13},{... | collective-permute-start | bytes 2359304 | tf_op jit(solution)/shard_map/while/body/eval_jaxpr/ppermute | solution.py:29
  171.4 13.4 collective-permute-start
  188.5 35.8 %collective-permute-start = (bf16[512,768]{1,0:T(8,128)(2,1)S(1)}, bf16[512,768]{1,0:T(8,128)(2,1)S(1)}, u32[]{:S(2)}, u32[]{:S(2)}) collective-permute-start(bf16[512,768]{1,0:T(8,128)(2,1)S(1)} %get-tuple-element.1431), channel_id=1, source_target_pairs={{0,1},{1,2},{2,3},{4,5},{5,6},{6,7},{8,9},{9,10},{10,11},{12,13},{... | collective-permute-start | bytes 2359304 | tf_op jit(solution)/shard_map/while/body/eval_jaxpr/ppermute | solution.py:29
  250.3 31.8 %collective-permute-start.1 = (bf16[512,768]{1,0:T(8,128)(2,1)}, bf16[512,768]{1,0:T(8,128)(2,1)S(1)}, u32[]{:S(2)}, u32[]{:S(2)}) collective-permute-start(bf16[512,768]{1,0:T(8,128)(2,1)} %get-tuple-element.1264), channel_id=1, source_target_pairs={{1,0},{2,1},{3,2},{5,4},{6,5},{7,6},{9,8},{10,9},{11,10},{13,12},{... | collective-permute-start | bytes 2359304 | tf_op jit(solution)/shard_map/while/body/eval_jaxpr/ppermute | solution.py:29
  271.3 9.7 copy-start.21
  271.4 9.7 copy-start.15
  271.4 9.7 copy-start.18
  290.9 37.0 %collective-permute-start.1 = (bf16[512,768]{1,0:T(8,128)(2,1)}, bf16[512,768]{1,0:T(8,128)(2,1)S(1)}, u32[]{:S(2)}, u32[]{:S(2)}) collective-permute-start(bf16[512,768]{1,0:T(8,128)(2,1)} %get-tuple-element.1264), channel_id=1, source_target_pairs={{1,0},{2,1},{3,2},{5,4},{6,5},{7,6},{9,8},{10,9},{11,10},{13,12},{... | collective-permute-start | bytes 2359304 | tf_op jit(solution)/shard_map/while/body/eval_jaxpr/ppermute | solution.py:29
  314.4 12.3 copy-start.21
  314.4 12.4 copy-start.15
  314.4 12.4 copy-start.18
  336.7 155.3 %collective-permute-start.1 = (bf16[512,768]{1,0:T(8,128)(2,1)}, bf16[512,768]{1,0:T(8,128)(2,1)S(1)}, u32[]{:S(2)}, u32[]{:S(2)}) collective-permute-start(bf16[512,768]{1,0:T(8,128)(2,1)} %get-tuple-element.1264), channel_id=1, source_target_pairs={{1,0},{2,1},{3,2},{5,4},{6,5},{7,6},{9,8},{10,9},{11,10},{13,12},{... | collective-permute-start | bytes 2359304 | tf_op jit(solution)/shard_map/while/body/eval_jaxpr/ppermute | solution.py:29
  360.2 12.3 copy-start.21
  360.2 12.4 copy-start.15
  360.2 12.4 copy-start.18
  372.5 119.4 %copy-start.22 = (f32[768]{0:T(1024)}, f32[768]{0:T(1024)S(1)}, u32[]{:S(2)}) copy-start(f32[768]{0:T(1024)S(1)} %select_add_fusion.11) | copy-start | bytes 9220 | tf_op jit(solution)/shard_map/while
  372.6 119.4 %copy-start.16 = (f32[768]{0:T(1024)}, f32[768]{0:T(1024)S(1)}, u32[]{:S(2)}) copy-start(f32[768]{0:T(1024)S(1)} %get-tuple-element.1407) | copy-start | bytes 9220 | tf_op jit(solution)/shard_map/while
  372.6 119.4 %copy-start.19 = (f32[768]{0:T(1024)}, f32[768]{0:T(1024)S(1)}, u32[]{:S(2)}) copy-start(f32[768]{0:T(1024)S(1)} %get-tuple-element.1406) | copy-start | bytes 9220 | tf_op jit(solution)/shard_map/while
  504.8 11.2 copy-start.2
  532.9 12.7 copy-start.3
  570.4 23.3 %copy-start.1 = (f32[512,768]{1,0:T(8,128)S(1)}, f32[512,768]{1,0:T(8,128)}, u32[]{:S(2)}) copy-start(f32[512,768]{1,0:T(8,128)} %copy-done) | copy-start | bytes 4718596 | tf_op jit(solution)/shard_map/while/body/eval_jaxpr/cond
  608.7 55.2 %collective-permute-start.1 = (bf16[512,768]{1,0:T(8,128)(2,1)}, bf16[512,768]{1,0:T(8,128)(2,1)S(1)}, u32[]{:S(2)}, u32[]{:S(2)}) collective-permute-start(bf16[512,768]{1,0:T(8,128)(2,1)} %get-tuple-element.1264), channel_id=1, source_target_pairs={{1,0},{2,1},{3,2},{5,4},{6,5},{7,6},{9,8},{10,9},{11,10},{13,12},{... | collective-permute-start | bytes 2359304 | tf_op jit(solution)/shard_map/while/body/eval_jaxpr/ppermute | solution.py:29
  644.3 12.3 copy-start.21
  644.3 12.4 copy-start.15
  644.3 12.4 copy-start.18
  676.8 11.2 copy-start.2
  704.9 12.8 copy-start.3
  742.5 23.3 %copy-start.1 = (f32[512,768]{1,0:T(8,128)S(1)}, f32[512,768]{1,0:T(8,128)}, u32[]{:S(2)}) copy-start(f32[512,768]{1,0:T(8,128)} %copy-done) | copy-start | bytes 4718596 | tf_op jit(solution)/shard_map/while/body/eval_jaxpr/cond
  780.5 50.8 %collective-permute-start.1 = (bf16[512,768]{1,0:T(8,128)(2,1)}, bf16[512,768]{1,0:T(8,128)(2,1)S(1)}, u32[]{:S(2)}, u32[]{:S(2)}) collective-permute-start(bf16[512,768]{1,0:T(8,128)(2,1)} %get-tuple-element.1264), channel_id=1, source_target_pairs={{1,0},{2,1},{3,2},{5,4},{6,5},{7,6},{9,8},{10,9},{11,10},{13,12},{... | collective-permute-start | bytes 2359304 | tf_op jit(solution)/shard_map/while/body/eval_jaxpr/ppermute | solution.py:29
  816.4 12.3 copy-start.21
  816.4 12.4 copy-start.15
  816.4 12.4 copy-start.18
  844.2 11.2 copy-start.2
  872.3 12.5 copy-start.3
  909.7 23.3 %copy-start.1 = (f32[512,768]{1,0:T(8,128)S(1)}, f32[512,768]{1,0:T(8,128)}, u32[]{:S(2)}) copy-start(f32[512,768]{1,0:T(8,128)} %copy-done) | copy-start | bytes 4718596 | tf_op jit(solution)/shard_map/while/body/eval_jaxpr/cond
  947.9 50.3 %collective-permute-start.1 = (bf16[512,768]{1,0:T(8,128)(2,1)}, bf16[512,768]{1,0:T(8,128)(2,1)S(1)}, u32[]{:S(2)}, u32[]{:S(2)}) collective-permute-start(bf16[512,768]{1,0:T(8,128)(2,1)} %get-tuple-element.1264), channel_id=1, source_target_pairs={{1,0},{2,1},{3,2},{5,4},{6,5},{7,6},{9,8},{10,9},{11,10},{13,12},{... | collective-permute-start | bytes 2359304 | tf_op jit(solution)/shard_map/while/body/eval_jaxpr/ppermute | solution.py:29
  983.5 12.3 copy-start.21
  983.5 12.4 copy-start.15
  983.5 12.4 copy-start.18
  999.9 573.1 %copy-start.20 = (f32[768]{0:T(1024)S(1)}, f32[768]{0:T(1024)}, u32[]{:S(2)}) copy-start(f32[768]{0:T(1024)} %get-tuple-element.845) | copy-start | bytes 9220
  1000.0 573.1 %copy-start.17 = (f32[768]{0:T(1024)S(1)}, f32[768]{0:T(1024)}, u32[]{:S(2)}) copy-start(f32[768]{0:T(1024)} %get-tuple-element.846) | copy-start | bytes 9220
  1000.0 573.1 %copy-start.23 = (f32[768]{0:T(1024)S(1)}, f32[768]{0:T(1024)}, u32[]{:S(2)}) copy-start(f32[768]{0:T(1024)} %get-tuple-element.844) | copy-start | bytes 9220
  1571.7 20.1 %collective-permute-start.3 = (bf16[1536,768]{1,0:T(8,128)(2,1)S(1)}, bf16[1536,768]{1,0:T(8,128)(2,1)}, u32[]{:S(2)}, u32[]{:S(2)}) collective-permute-start(bf16[1536,768]{1,0:T(8,128)(2,1)S(1)} %slice.77), channel_id=1, source_target_pairs={{1,0},{2,1},{3,2},{5,4},{6,5},{7,6},{9,8},{10,9},{11,10},{13,12},{... | collective-permute-start | bytes 7077896 | tf_op jit(solution)/shard_map/ppermute | solution.py:29
  (38 other events, 145.4 us)
Sparse Core Ops, SparseCore 0:
  1000.1 568.9 all-reduce.5
where the time goes:
time: 1640 us; the launch traced here: 1610 us
  waiting for transfers between devices  697 us (42%)
  matrix products  333 us (20%)
  other arithmetic  226 us (14%)
  local copies, waits for them, and re-layouts  166 us (10%)
  starting transfers between devices  112 us (7%)
  loops' own time  42.6 us (3%)
  blocking collectives  18.7 us (1%)
    psum x1, waiting for transfers between devices, on_device(): lax.psum((grad_main, grad_down, grad_bias, grad_gain, grad_shift), 'dp')  569 us
    add x24, other arithmetic, backward_step(): running_total + summand_value  140 us
    ppermute x14, waiting for transfers between devices, passed_along(): return lax.ppermute(block, axis, route)  128 us
    ppermute x14, starting transfers between devices, passed_along(): return lax.ppermute(block, axis, route)  111 us
    another operation x35, local copies, waits for them, and re-layouts  58.5 us
    dot_general x3, matrix products, attend_input(): jnp.einsum('hqk,qhd->khd', grad_scores, query_heads, preferred_element_ty...  56 us
    sub x6, matrix products, attention_parts(): soft_full = jax.nn.softmax(scores, axis=-1)  55.9 us
    dot_general x3, matrix products, attend_input(): jnp.einsum('hqk,khd->qhd', grad_scores, key_heads, preferred_element_type...  55.6 us
  transfers between devices with their start and end apart: 15, of which 5 were waited for; matrix products, arithmetic and copies ran while one was open for 16% of the time, Pallas kernels for 0%

commit v1 on v0

v1 whole, which is shorter than its diff:
```python
from functools import partial

import jax
import jax.numpy as jnp
from jax import lax
from jax.experimental import pallas as pl
from jax.experimental.pallas import tpu as pltpu
from jax.sharding import PartitionSpec as P

HEAD = 64
NORM_EPS = 1e-06
MASK_FILL = -1000000000.0
MESH = pl.DeviceIdType.MESH
BF = jnp.bfloat16
F32 = jnp.float32
MIB = 1024 * 1024
NN = (((1,), (0,)), ((), ()))
NT = (((1,), (1,)), ((), ()))
TN = (((0,), (0,)), ((), ()))
LN_ROWS = 64
W_ORDER = (1, 2, 0, 3)


def mm(a, b, dims=NN):
    return lax.dot_general(a, b, dims, preferred_element_type=F32)


def gelu_pair(x):
    ax = jnp.abs(x)
    t = 1.0 / (1.0 + ax * (0.3275911 * 0.7071067811865476))
    e = jnp.exp(x * x * -0.5)
    poly = ((((0.5 * 1.061405429) * t + (0.5 * -1.453152027)) * t + (0.5 * 1.421413741)) * t + (0.5 * -0.284496736)) * t + (0.5 * 0.254829592)
    tail = poly * t * e
    cdf = jnp.where(x >= 0.0, 1.0 - tail, tail)
    return x * cdf, cdf + x * (e * 0.3989422804014327)


def layer_kernel(
    tok, cot, lens, wm, wd, vec,
    out_ref, ing_ref, g_ref, small_ref,
    W, W2, V, L, R, Q, KV, N, RS, LSE, H2, GIN, GMID, GOUT, RES, DCTX, DKV, DKVR, GR, GS, VR,
    sem_w, sem_tok, sem_cot, send_w, recv_w, send_kv, recv_kv, send_h, recv_h, sem_o, recv_o,
    send_dkv, recv_dkv, send_g, recv_g, sem_i, recv_i, send_gr, recv_gr, sem_go, send_v, recv_v,
):
    nq, seq_len, D = tok.shape
    half = seq_len // 2
    pairs = D // 128
    dp = lax.axis_index("dp")
    s = lax.axis_index("section")
    p = lax.rem(s, 2)
    layer = s // 2
    partner = (dp, s + 1 - 2 * p)
    across = (dp, lax.rem(s + 2, 4))
    first = layer == 0
    last = layer == 1
    own = pl.ds(pl.multiple_of(p * half, half), half)
    other = pl.ds(pl.multiple_of((1 - p) * half, half), half)

    def rows(q):
        return pl.ds(pl.multiple_of(q * half, half), half)

    def copy_w(b):
        return pltpu.make_async_copy(wm.at[:, pl.ds(b * D, D)], W.at[p, b], sem_w.at[b])

    def copy_w2(b):
        return pltpu.make_async_copy(wd.at[pl.ds(b * D, D), :], W2.at[2 * p + b], sem_w.at[4 + b])

    def copy_tok(q):
        return pltpu.make_async_copy(tok.at[q, own], L.at[0, rows(q)], sem_tok.at[q])

    def copy_cot(q):
        return pltpu.make_async_copy(cot.at[q, own], GIN.at[q], sem_cot.at[q])

    @pl.when(first)
    def _():
        for q in range(nq):
            copy_tok(q).start()

    for b in W_ORDER:
        copy_w(b).start()
    for b in range(2):
        copy_w2(b).start()

    @pl.when(last)
    def _():
        for q in range(nq):
            copy_cot(q).start()

    barrier = pltpu.get_barrier_semaphore()
    for peer in (partner, across):
        pl.semaphore_signal(barrier, inc=1, device_id=peer, device_id_type=MESH)
    pl.semaphore_wait(barrier, 2)

    def remote(src, dst, send, recv, dev):
        return pltpu.make_async_remote_copy(
            src_ref=src, dst_ref=dst, send_sem=send, recv_sem=recv, device_id=dev, device_id_type=MESH
        )

    def send_weights(b):
        return remote(wm.at[:, pl.ds(b * D, D)], W.at[p, b], send_w.at[b], recv_w.at[b], partner)

    def send_weights2(b):
        return remote(wd.at[pl.ds(b * D, D), :], W2.at[2 * p + b], send_w.at[4 + b], recv_w.at[4 + b], partner)

    def send_vec():
        return remote(vec, VR, send_v, recv_v, partner)

    send_vec().start()
    for b in W_ORDER:
        send_weights(b).start()
    for b in range(2):
        send_weights2(b).start()

    def need_w(sec, b):
        @pl.when(p == sec)
        def _():
            copy_w(b).wait()

        @pl.when(p != sec)
        def _():
            remote(wm.at[:, pl.ds(b * D, D)], W.at[1 - p, b], send_w.at[b], recv_w.at[b], partner).wait_recv()

    def need_w2():
        for b in range(2):
            copy_w2(b).wait()
            remote(
                wd.at[pl.ds(b * D, D), :], W2.at[2 * (1 - p) + b], send_w.at[4 + b], recv_w.at[4 + b], partner
            ).wait_recv()

    def send_keys(q):
        return remote(KV.at[q, own], KV.at[q, own], send_kv.at[q], recv_kv.at[q], partner)

    def take_keys(q):
        return remote(KV.at[q, other], KV.at[q, other], send_kv.at[q], recv_kv.at[q], partner)

    def hand_on(q):
        return remote(H2.at[q], L.at[0, rows(q)], send_h.at[q], recv_h.at[q], across)

    def hand_back(q):
        return remote(GOUT.at[q], GIN.at[q], send_g.at[q], recv_g.at[q], across)

    def put(src, dst_ref, q, sec, sems, recvs):
        keep = pltpu.make_async_copy(src, dst_ref.at[q, own], sems.at[sec, q])
        give = remote(src, dst_ref.at[q, own], sems.at[sec, q], recvs.at[q], partner)
        return keep, give

    def put_start(src, dst_ref, q, sec, sems, recvs):
        keep, give = put(src, dst_ref, q, sec, sems, recvs)

        @pl.when(p == sec)
        def _():
            keep.start()

        @pl.when(p != sec)
        def _():
            give.start()

    def put_wait(src, dst_ref, q, sec, sems, recvs):
        keep, give = put(src, dst_ref, q, sec, sems, recvs)

        @pl.when(p == sec)
        def _():
            keep.wait()
            remote(src, dst_ref.at[q, other], sems.at[sec, q], recvs.at[q], partner).wait_recv()

        @pl.when(p != sec)
        def _():
            give.wait_send()

    lane = lax.broadcasted_iota(jnp.int32, (1, 128), 1)
    low_lanes = (lane < HEAD).astype(F32)
    high_lanes = 1.0 - low_lanes

    def split_lanes(x):
        wide = x.astype(F32)
        return (wide * low_lanes).astype(BF), (wide * high_lanes).astype(BF)

    key_row = lax.broadcasted_iota(jnp.int32, (seq_len, half), 0)

    def norm_forward(sec, h_ref_at, dst, q):
        bias, gain, shift = V[sec, 0:1, :], V[sec, 1:2, :], V[sec, 2:3, :]

        def body(i, c):
            r = pl.ds(pl.multiple_of(i * LN_ROWS, LN_ROWS), LN_ROWS)
            rq = pl.ds(pl.multiple_of(q * half + i * LN_ROWS, LN_ROWS), LN_ROWS)
            residual = L[h_ref_at, rq, :].astype(F32) + (RES[r, :] + bias)
            center = jnp.mean(residual, axis=-1, keepdims=True)
            centred = residual - center
            spread = jnp.mean(centred * centred, axis=-1, keepdims=True)
            rstd = lax.rsqrt(spread + NORM_EPS)
            normed = centred * rstd
            N[sec, rq, :] = normed.astype(BF)
            RS[sec, rq, :] = jnp.broadcast_to(rstd, (LN_ROWS, 128))
            dst(r, rq, (normed * gain + shift).astype(BF))
            return c

        lax.fori_loop(0, half // LN_ROWS, body, 0)

    def norm_backward(sec, g_ref, at, q):
        gain = V[sec, 1:2, :]

        def body(i, c):
            r = pl.ds(pl.multiple_of(i * LN_ROWS, LN_ROWS), LN_ROWS)
            rq = pl.ds(pl.multiple_of(q * half + i * LN_ROWS, LN_ROWS), LN_ROWS)
            g = g_ref[q, r, :].astype(F32)
            normed = N[sec, rq, :].astype(F32)
            rstd = RS[sec, rq, 0:1]
            gg = g * gain
            first_mean = jnp.mean(gg, axis=-1, keepdims=True)
            second_mean = jnp.mean(gg * normed, axis=-1, keepdims=True)
            dres = rstd * (gg - first_mean - normed * second_mean)
            RES[r, :] = dres
            R[at, rq, :] = dres.astype(BF)
            b, a, t = c
            return (
                b + jnp.sum(dres, axis=0, keepdims=True),
                a + jnp.sum(g * normed, axis=0, keepdims=True),
                t + jnp.sum(g, axis=0, keepdims=True),
            )

        zero = jnp.zeros((1, D), F32)
        b, a, t = lax.fori_loop(0, half // LN_ROWS, body, (zero, zero, zero))
        small_ref[sec, 0:1, :] += b
        small_ref[sec, 1:2, :] += a
        small_ref[sec, 2:3, :] += t

    small_ref[...] = jnp.zeros_like(small_ref)

    def forward(q, carry):
        length = lens[q]

        @pl.when(first)
        def _():
            copy_tok(q).wait()

        @pl.when(last)
        def _():
            hand_on(q).wait_recv()

        @pl.when(q == 0)
        def _():
            need_w(0, 1)

        h = L[0, rows(q), :]
        KV[q, own, 0:D] = mm(h, W[0, 1]).astype(BF)

        @pl.when(q == 0)
        def _():
            need_w(0, 2)

        KV[q, own, D : 2 * D] = mm(h, W[0, 2]).astype(BF)
        send_keys(q).start()

        @pl.when(q == 0)
        def _():
            need_w(0, 0)

        Q[rows(q), :] = (mm(h, W[0, 0]) * HEAD ** (-0.5)).astype(BF)
        take_keys(q).wait_recv()
        valid = key_row < length

        def heads(hp, c):
            cols = pl.ds(pl.multiple_of(hp * 128, 128), 128)
            vcols = pl.ds(pl.multiple_of(D + hp * 128, 128), 128)
            kp = KV[q, :, cols]
            v_t = jnp.transpose(KV[q, :, vcols])
            done = []
            for i, qh in enumerate(split_lanes(Q[rows(q), cols])):
                st = jnp.where(valid, mm(kp, qh, NT), MASK_FILL)
                top = jnp.max(st, axis=0, keepdims=True)
                e = jnp.exp(st - top)
                total = jnp.sum(e, axis=0, keepdims=True)
                LSE[q, 2 * hp + i] = top + jnp.log(total)
                ct = mm(v_t[i * HEAD : (i + 1) * HEAD, :], e.astype(BF))
                done.append(ct * (1.0 / total))
            L[1, rows(q), cols] = jnp.transpose(jnp.concatenate(done, axis=0)).astype(BF)
            return c

        lax.fori_loop(0, pairs, heads, 0)

        @pl.when(q == 0)
        def _():
            need_w(0, 3)
            send_vec().wait_recv()
            mine = vec[...]
            theirs = VR[...]

            @pl.when(p == 0)
            def _():
                V[0] = mine
                V[1] = theirs

            @pl.when(p == 1)
            def _():
                V[0] = theirs
                V[1] = mine

        RES[...] = mm(L[1, rows(q), :], W[0, 3])

        def keep_mid(r, rq, x):
            L[2, rq, :] = x

        norm_forward(0, 0, keep_mid, q)
        put_start(L.at[2, rows(q)], out_ref, q, 0, sem_o, recv_o)

        def up(b, c):
            for j in range(4):
                @pl.when((q == 0) & (b == j))
                def _():
                    need_w(1, j)
            hidden, slope = gelu_pair(mm(L[2, rows(q), :], W[1, b]))
            L[3 + b, rows(q), :] = hidden.astype(BF)
            R[5 + b, rows(q), :] = slope.astype(BF)
            return c

        lax.fori_loop(0, 4, up, 0)

        @pl.when(q == 0)
        def _():
            need_w2()

        for n in range(D // 256):
            c = slice(n * 256, (n + 1) * 256)
            acc = mm(L[3, rows(q), :], W2[0, :, c])
            for b in range(1, 4):
                acc += mm(L[3 + b, rows(q), :], W2[b, :, c])
            RES[:, c] = acc

        def keep_out(r, rq, x):
            H2[q, r, :] = x

        norm_forward(1, 2, keep_out, q)

        @pl.when(first)
        def _():
            hand_on(q).start()

        put_start(H2.at[q], out_ref, q, 1, sem_o, recv_o)
        return carry

    lax.fori_loop(0, nq, forward, 0)

    def send_dkeys(q):
        return remote(DKV.at[1 - p], DKVR.at[q], send_dkv.at[q], recv_dkv.at[q], partner)

    def backward(q, carry):
        length = lens[q]

        @pl.when(last)
        def _():
            copy_cot(q).wait()

        @pl.when(first)
        def _():
            hand_back(q).wait_recv()

        norm_backward(1, GIN, 4, q)

        def down(b, c):
            dh = mm(R[4, rows(q), :], W2[b], NT)
            R[5 + b, rows(q), :] = (dh * R[5 + b, rows(q), :].astype(F32)).astype(BF)
            return c

        lax.fori_loop(0, 4, down, 0)

        for n in range(D // 256):
            c = slice(n * 256, (n + 1) * 256)
            acc = RES[:, c]
            for b in range(4):
                acc += mm(R[5 + b, rows(q), :], W[1, b, c, :], NT)
            GMID[q, :, c] = acc.astype(BF)
        put_start(GMID.at[q], ing_ref, q, 1, sem_i, recv_i)

        norm_backward(0, GMID, 3, q)
        DCTX[...] = mm(R[3, rows(q), :], W[0, 3], NT).astype(BF)

        @pl.when(q > 0)
        def _():
            send_dkeys(q - 1).wait_send()

        valid = key_row < length

        def heads(hp, c):
            cols = pl.ds(pl.multiple_of(hp * 128, 128), 128)
            vcols = pl.ds(pl.multiple_of(D + hp * 128, 128), 128)
            kp = KV[q, :, cols]
            vp = KV[q, :, vcols]
            qp = Q[rows(q), cols]
            dcp = DCTX[:, cols]
            k_t = jnp.transpose(kp)
            dqs, dks, dvs = [], [], []
            for i, (qh, dch) in enumerate(zip(split_lanes(qp), split_lanes(dcp))):
                st = jnp.where(valid, mm(kp, qh, NT), MASK_FILL)
                prob = jnp.exp(st - LSE[q, 2 * hp + i])
                dprob = mm(vp, dch, NT)
                mean = jnp.sum(prob * dprob, axis=0, keepdims=True)
                ds = (prob * (dprob - mean)).astype(BF)
                dvs.append(mm(prob.astype(BF), dcp))
                dks.append(mm(ds, qp))
                dqs.append(mm(k_t[i * HEAD : (i + 1) * HEAD, :], ds))
            dq = jnp.concatenate(dqs, axis=0) * HEAD ** (-0.5)
            R[0, rows(q), cols] = jnp.transpose(dq).astype(BF)
            low = lane < HEAD
            dk = jnp.where(low, dks[0], dks[1]).astype(BF)
            dv = jnp.where(low, dvs[0], dvs[1]).astype(BF)
            DKV[0, :, cols] = dk[:half]
            DKV[1, :, cols] = dk[half:]
            DKV[0, :, vcols] = dv[:half]
            DKV[1, :, vcols] = dv[half:]
            return c

        lax.fori_loop(0, pairs, heads, 0)
        send_dkeys(q).start()
        for n in range(D // 256):
            c = slice(n * 256, (n + 1) * 256)
            RES[:, c] = RES[:, c] + mm(R[0, rows(q), :], W[0, 0, c, :], NT)
        send_dkeys(q).wait_recv()
        R[1, rows(q), :] = (DKV[p, :, 0:D].astype(F32) + DKVR[q, :, 0:D].astype(F32)).astype(BF)
        R[2, rows(q), :] = (DKV[p, :, D : 2 * D].astype(F32) + DKVR[q, :, D : 2 * D].astype(F32)).astype(BF)
        for n in range(D // 256):
            c = slice(n * 256, (n + 1) * 256)
            acc = RES[:, c]
            for b in range(1, 3):
                acc += mm(R[b, rows(q), :], W[0, b, c, :], NT)
            GOUT[q, :, c] = acc.astype(BF)

        @pl.when(last)
        def _():
            hand_back(q).start()

        put_start(GOUT.at[q], ing_ref, q, 0, sem_i, recv_i)
        return carry

    lax.fori_loop(0, nq, backward, 0)

    left = ((0, 0, 0, 1, 3, 4), (2, 2, 2, 2, 5, 6))
    right = ((0, 1, 2, 3, 4, 4), (5, 6, 7, 8, 4, 4))

    def pick(table, sec, j):
        return table[0][j] + sec * (table[1][j] - table[0][j])

    def send_grad(j):
        return remote(GS.at[j % 2], GR.at[j], send_gr.at[j], recv_gr.at[j], partner)

    def store_grad(j):
        return pltpu.make_async_copy(GR.at[j], g_ref.at[j], sem_go.at[j])

    for j in range(6):
        li, ri = pick(left, 1 - p, j), pick(right, 1 - p, j)
        if j >= 2:
            send_grad(j - 2).wait_send()
        for n in range(D // 256):
            c = slice(n * 256, (n + 1) * 256)
            GS[j % 2, :, c] = mm(L[li], R[ri, :, c], TN).astype(BF)
        send_grad(j).start()
    for j in range(6):
        li, ri = pick(left, p, j), pick(right, p, j)
        send_grad(j).wait_recv()
        for n in range(D // 256):
            c = slice(n * 256, (n + 1) * 256)
            GR[j, :, c] = (mm(L[li], R[ri, :, c], TN) + GR[j, :, c].astype(F32)).astype(BF)
        store_grad(j).start()

    for j in range(4, 6):
        send_grad(j).wait_send()
    for j in range(6):
        store_grad(j).wait()
    send_vec().wait_send()
    for b in range(4):
        send_weights(b).wait_send()
    for b in range(2):
        send_weights2(b).wait_send()
    send_dkeys(nq - 1).wait_send()
    for q in range(nq):
        send_keys(q).wait_send()

        @pl.when(first)
        def _():
            hand_on(q).wait_send()

        @pl.when(last)
        def _():
            hand_back(q).wait_send()

        put_wait(L.at[2, rows(q)], out_ref, q, 0, sem_o, recv_o)
        put_wait(H2.at[q], out_ref, q, 1, sem_o, recv_o)
        put_wait(GMID.at[q], ing_ref, q, 1, sem_i, recv_i)
        put_wait(GOUT.at[q], ing_ref, q, 0, sem_i, recv_i)


def run_layers(tokens, cotangent, lengths, weights, w_down, vec):
    nq, seq_len, D = tokens.shape
    half = seq_len // 2
    tall = nq * half
    dma = pltpu.SemaphoreType.DMA
    any_spec = pl.BlockSpec(memory_space=pl.ANY)
    vmem_spec = pl.BlockSpec(memory_space=pltpu.VMEM)
    return pl.pallas_call(
        layer_kernel,
        name="layers",
        out_shape=(
            jax.ShapeDtypeStruct((nq, seq_len, D), BF),
            jax.ShapeDtypeStruct((nq, seq_len, D), BF),
            jax.ShapeDtypeStruct((6, D, D), BF),
            jax.ShapeDtypeStruct((2, 8, D), F32),
        ),
        in_specs=[any_spec, any_spec, pl.BlockSpec(memory_space=pltpu.SMEM), any_spec, any_spec, vmem_spec],
        out_specs=(any_spec, any_spec, any_spec, vmem_spec),
        scratch_shapes=[
            pltpu.VMEM((2, 4, D, D), BF),
            pltpu.VMEM((4, D, D), BF),
            pltpu.VMEM((2, 8, D), F32),
            pltpu.VMEM((7, tall, D), BF),
            pltpu.VMEM((9, tall, D), BF),
            pltpu.VMEM((tall, D), BF),
            pltpu.VMEM((nq, seq_len, 2 * D), BF),
            pltpu.VMEM((2, tall, D), BF),
            pltpu.VMEM((2, tall, 128), F32),
            pltpu.VMEM((nq, D // HEAD, 1, half), F32),
            pltpu.VMEM((nq, half, D), BF),
            pltpu.VMEM((nq, half, D), BF),
            pltpu.VMEM((nq, half, D), BF),
            pltpu.VMEM((nq, half, D), BF),
            pltpu.VMEM((half, D), F32),
            pltpu.VMEM((half, D), BF),
            pltpu.VMEM((2, half, 2 * D), BF),
            pltpu.VMEM((nq, half, 2 * D), BF),
            pltpu.VMEM((6, D, D), BF),
            pltpu.VMEM((2, D, D), BF),
            pltpu.VMEM((8, D), F32),
            dma((6,)), dma((nq,)), dma((nq,)), dma((6,)), dma((6,)),
            dma((nq,)), dma((nq,)), dma((nq,)), dma((nq,)), dma((2, nq)), dma((nq,)),
            dma((nq,)), dma((nq,)), dma((nq,)), dma((nq,)), dma((2, nq)), dma((nq,)),
            dma((6,)), dma((6,)), dma((6,)), dma, dma,
        ],
        compiler_params=pltpu.CompilerParams(
            collective_id=0, has_side_effects=True, vmem_limit_bytes=63 * MIB
        ),
        cost_estimate=pl.CostEstimate(flops=60 * 10**9, bytes_accessed=40 * 10**6, transcendentals=10**7),
    )(tokens, cotangent, lengths, weights, w_down, vec)


CLASS_ROWS = (112, 112, 160)
CLASS_AT = (0, 112, 224)
STEP_ROWS = 384
LAG = 4


def sum_kernel(line, g_ref, small_in, fin_ref, small_out, G, RV, FIN, SR, sem_in, sem_out, s_up, s_down, r_up, r_fin, t_up, t_down, q_up, q_fin):
    blocks, D, _ = g_ref.shape
    steps = blocks * D // STEP_ROWS
    per = D // STEP_ROWS
    dp = lax.axis_index("dp")
    s = lax.axis_index("section")
    y = lax.rem(dp, 2)
    z = dp // 2
    has_dn = z > 0
    has_up = z < line - 1
    side = (dp + 1 - 2 * y, s)
    below = (lax.rem(dp + 2 * line - 2, 2 * line), s)
    above = (lax.rem(dp + 2, 2 * line), s)
    peers = (side, below, above)

    def load(b):
        return pltpu.make_async_copy(g_ref.at[b], G.at[b], sem_in.at[b])

    def store(b):
        return pltpu.make_async_copy(FIN.at[b], fin_ref.at[b], sem_out.at[b])

    for b in range(blocks):
        load(b).start()

    barrier = pltpu.get_barrier_semaphore()
    pl.semaphore_signal(barrier, inc=1, device_id=side, device_id_type=MESH)

    @pl.when(has_dn)
    def _():
        pl.semaphore_signal(barrier, inc=1, device_id=below, device_id_type=MESH)

    @pl.when(has_up)
    def _():
        pl.semaphore_signal(barrier, inc=1, device_id=above, device_id_type=MESH)

    pl.semaphore_wait(barrier, 1 + has_dn.astype(jnp.int32) + has_up.astype(jnp.int32))

    def roles(kind, k):
        if kind < 2:
            rail = y == kind
            return (
                (rail, rail & (z <= k) & has_dn, rail & (z >= k) & has_up),
                (jnp.logical_not(rail), rail & (z > k), rail & (z < k)),
            )
        at = z == k
        return (
            (at & (y == 0), (z <= k) & has_dn, (z >= k) & has_up),
            (at & (y == 1), z > k, z < k),
        )

    def root_of(kind, i):
        if kind < 2:
            return line // 2 - 1 + lax.rem(i, 2)
        return lax.rem(line // 2 - 1 + i, line)

    def rem_copy(src, dst, send, recv, dev):
        return pltpu.make_async_remote_copy(
            src_ref=src, dst_ref=dst, send_sem=send, recv_sem=recv, device_id=dev, device_id_type=MESH
        )

    slot_at_parent = (0, 2, 1)

    def tree(kids, parents, acc, slots, fin, sup, sdown, rup, rfin):
        def add_children():
            for n in range(3):
                @pl.when(kids[n])
                def _():
                    rem_copy(slots(n), slots(n), sup, rup(n), peers[n]).wait_recv()
                    acc[...] = (acc[...].astype(F32) + slots(n)[...].astype(F32)).astype(acc.dtype)

        def send_up(wait):
            for n in range(3):
                @pl.when(parents[n])
                def _():
                    c = rem_copy(acc, slots(slot_at_parent[n]), sup, rup(slot_at_parent[n]), peers[n])
                    c.wait_send() if wait else c.start()

        root = jnp.logical_not(parents[0] | parents[1] | parents[2])

        def finish_root():
            @pl.when(root)
            def _():
                fin[...] = acc[...]

        def wait_final():
            @pl.when(jnp.logical_not(root))
            def _():
                rem_copy(acc, fin, sup, rfin, peers[0]).wait_recv()

        def send_down(wait):
            for n in range(3):
                @pl.when(kids[n])
                def _():
                    c = rem_copy(fin, fin, sdown(n), rfin, peers[n])
                    c.wait_send() if wait else c.start()

        return root, add_children, send_up, finish_root, wait_final, send_down

    def chunk(kind, i):
        b = i // per
        at = pl.multiple_of(lax.rem(i, per) * STEP_ROWS + CLASS_AT[kind], 16)
        r = pl.ds(at, CLASS_ROWS[kind])
        kids, parents = roles(kind, root_of(kind, i))
        return tree(
            kids, parents, G.at[b, r], lambda n: RV.at[n, b, r], FIN.at[b, r],
            s_up.at[kind, i], lambda n: s_down.at[kind, n, i], lambda n: r_up.at[kind, n, i], r_fin.at[kind, i],
        )

    def up(i):
        @pl.when(lax.rem(i, per) == 0)
        def _():
            load(i // per).wait()

        for kind in range(3):
            root, add_children, send_up, finish_root, wait_final, send_down = chunk(kind, i)
            add_children()
            send_up(False)
            finish_root()

            @pl.when(root)
            def _():
                send_down(False)

    def down(i):
        for kind in range(3):
            root, add_children, send_up, finish_root, wait_final, send_down = chunk(kind, i)
            wait_final()

            @pl.when(jnp.logical_not(root))
            def _():
                send_down(False)

        @pl.when(lax.rem(i, per) == per - 1)
        def _():
            store(i // per).start()

    SR[3] = small_in[...]
    kids, parents = roles(0, line // 2)
    little = tree(
        kids, parents, SR.at[3], lambda n: SR.at[n], SR.at[4], t_up, lambda n: t_down.at[n], lambda n: q_up.at[n], q_fin
    )
    little[1]()
    little[2](False)
    little[3]()

    @pl.when(little[0])
    def _():
        little[5](False)

    def step(i, c):
        @pl.when(i < steps)
        def _():
            up(i)

        @pl.when(i >= LAG)
        def _():
            down(i - LAG)

        return c

    lax.fori_loop(0, steps + LAG, step, 0)
    little[4]()

    @pl.when(jnp.logical_not(little[0]))
    def _():
        little[5](False)

    small_out[...] = SR[4]

    def drain(i, c):
        for kind in range(3):
            t = chunk(kind, i)
            t[2](True)
            t[5](True)
        return c

    lax.fori_loop(0, steps, drain, 0)
    little[2](True)
    little[5](True)
    for b in range(blocks):
        store(b).wait()


def sum_over_dp(grads, small):
    blocks, D, _ = grads.shape
    steps = blocks * D // STEP_ROWS
    line = lax.axis_size("dp") // 2
    dma = pltpu.SemaphoreType.DMA
    any_spec = pl.BlockSpec(memory_space=pl.ANY)
    vmem_spec = pl.BlockSpec(memory_space=pltpu.VMEM)
    return pl.pallas_call(
        partial(sum_kernel, line),
        name="sum_over_dp",
        out_shape=(
            jax.ShapeDtypeStruct(grads.shape, BF),
            jax.ShapeDtypeStruct(small.shape, F32),
        ),
        in_specs=[any_spec, vmem_spec],
        out_specs=(any_spec, vmem_spec),
        scratch_shapes=[
            pltpu.VMEM((blocks, D, D), BF),
            pltpu.VMEM((3, blocks, D, D), BF),
            pltpu.VMEM((blocks, D, D), BF),
            pltpu.VMEM((5,) + small.shape, F32),
            dma((blocks,)), dma((blocks,)),
            dma((3, steps)), dma((3, 3, steps)), dma((3, 3, steps)), dma((3, steps)),
            dma, dma((3,)), dma((3,)), dma,
        ],
        compiler_params=pltpu.CompilerParams(
            collective_id=1, has_side_effects=True, vmem_limit_bytes=60 * MIB
        ),
        cost_estimate=pl.CostEstimate(flops=10**7, bytes_accessed=30 * 10**6, transcendentals=0),
    )(grads, small)


def on_device(tokens, lengths, w_main, w_down_half, out_bias, ln_gain, ln_bias, cotangent):
    D = tokens.shape[-1]
    s = lax.axis_index("section")
    p = lax.rem(s, 2)
    vec = jnp.concatenate([out_bias, ln_gain, ln_bias, jnp.zeros((5, D), F32)], axis=0)
    kept_out, kept_grad, grads, small = run_layers(tokens, cotangent, lengths, w_main[0], w_down_half[0], vec)
    mine = lax.dynamic_index_in_dim(small, p, 0, keepdims=False)
    theirs = lax.dynamic_index_in_dim(small, 1 - p, 0, keepdims=False)
    pairs = [(i, i + 1 - 2 * (i % 2)) for i in range(lax.axis_size("section"))]
    small = mine + lax.ppermute(theirs, "section", pairs)
    total, small = sum_over_dp(grads, small)
    grad_main = jnp.swapaxes(total[:4], 0, 1).reshape(D, 4 * D).astype(F32)
    grad_half = total[4:].reshape(2 * D, D).astype(F32)
    return (
        kept_out[None],
        kept_grad[None],
        grad_main[None],
        grad_half[None],
        small[0:1],
        small[1:2],
        small[2:3],
    )


def solution(mesh):
    in_specs = (
        P("dp", None, None),
        P("dp"),
        P("section", None, None),
        P("section", None, None),
        P("section", None),
        P("section", None),
        P("section", None),
        P("dp", None, None),
    )
    out_specs = (
        P("section", "dp", None, None),
        P("section", "dp", None, None),
        P("section", None, None),
        P("section", None, None),
        P("section", None),
        P("section", None),
        P("section", None),
    )
    return jax.shard_map(
        on_device, mesh=mesh, in_specs=in_specs, out_specs=out_specs, check_vma=False
    )
```

time: 1640 us -> 776 us (0.47); the launches traced: 1610 us -> 768 us
  Pallas kernels: 0 us -> 727 us
  waiting for transfers between devices: 697 us -> 1.08 us
  matrix products: 333 us -> 0 us
  other arithmetic: 226 us -> 12.2 us
  local copies, waits for them, and re-layouts: 166 us -> 27.4 us
  starting transfers between devices: 112 us -> 0.12 us
  loops' own time: 42.6 us -> 0 us
  blocking collectives: 18.7 us -> 0 us
    pallas_call x0 -> x2, Pallas kernels: none -> 727 us  [the longest x1 545 us: sum_over_dp(): pl.pallas_call(partial(sum_kernel, line), name='sum_over_dp', out_shape=(...]
    psum x1 -> x0, waiting for transfers between devices: 569 us -> none  [on_device(): lax.psum((grad_main, grad_down, grad_bias, grad_gain, grad_shift), 'dp')]
    dot_general x42 -> x0, matrix products: 277 us -> none  [the longest x3 56 us: attend_input(): jnp.einsum('hqk,qhd->khd', grad_scores, query_heads, preferred_element_ty...]
    add x24 -> x1, other arithmetic: 140 us -> 1.35 us  [on_device(): small = mine + lax.ppermute(theirs, 'section', pairs)]
    ppermute x14 -> x1, waiting for transfers between devices: 128 us -> 1.08 us  [on_device(): small = mine + lax.ppermute(theirs, 'section', pairs)]
    ppermute x14 -> x1, starting transfers between devices: 111 us -> 0.12 us  [on_device(): small = mine + lax.ppermute(theirs, 'section', pairs)]
    another operation x35 -> x0, local copies, waits for them, and re-layouts: 58.5 us -> none
    sub x6 -> x0, matrix products: 55.9 us -> none  [attention_parts(): soft_full = jax.nn.softmax(scores, axis=-1)]
  transfers between devices with their start and end apart: 15 -> 1, of which waited for: 5 -> 1; matrix products, arithmetic and copies ran while one was open for 16% -> 0% of each run, Pallas kernels for 0% -> 0%
where the time goes in v1:
time: 776 us; the launch traced here: 768 us
  Pallas kernels  727 us (94%)
  local copies, waits for them, and re-layouts  27.4 us (4%)
  other arithmetic  12.2 us (2%)
    pallas_call x1, Pallas kernels, sum_over_dp(): pl.pallas_call(partial(sum_kernel, line), name='sum_over_dp', out_shape=(...  545 us
    pallas_call x1, Pallas kernels, run_layers(): pl.pallas_call(layer_kernel, name='layers', out_shape=(jax.ShapeDtypeStru...  181 us
  transfers between devices with their start and end apart: 1, of which 1 were waited for; matrix products, arithmetic and copies ran while one was open for 0% of the time, Pallas kernels for 0%

profile of v1, /device:TPU:4, one launch (start us, length us, event | category | flops | bytes accessed | tf_op | source)
XLA Modules:
  0.0 768.0 jit_solution(12549865430380968709)
XLA Ops:
  0.6 0.1 pad.3.clone
  0.7 1.4 maximum_maximum_fusion.vec
  2.1 181.1 %layers.1 = (bf16[3,512,768]{2,1,0:T(8,128)(2,1)}, bf16[3,512,768]{2,1,0:T(8,128)(2,1)}, bf16[6,768,768]{2,1,0:T(8,128)(2,1)}, f32[2,8,768]{2,1,0:T(8,128)}) custom-call(bf16[3,512,768]{2,1,0:T(8,128)(2,1)} %tok.1, bf16[3,512,768]{2,1,0:T(8,128)(2,1)} %cot.1, s32[3]{0:T(128)} %lens.1, bf16[768,3072]{1,0:T(8,128)(2,1)} %bitcast.19, ...), custom_call_target="tpu_custom_call" | custom-call | flops 60000002048 | bytes 40000000 | tf_op jit(solution)/shard_map/layers/pallas_call | solution.py:498
  183.3 0.7 dynamic-slice_bitcast_fusion
  184.0 0.1 collective-permute-start
  184.1 1.1 collective-permute-done
  185.2 1.4 bitcast_add_fusion.small_in
  186.6 545.5 %sum_over_dp.1 = (bf16[6,768,768]{2,1,0:T(8,128)(2,1)}, f32[8,768]{1,0:T(8,128)}) custom-call(bf16[6,768,768]{2,1,0:T(8,128)(2,1)} %get-tuple-element.15.g_ref, f32[8,768]{1,0:T(8,128)} %bitcast_add_fusion.small_in), custom_call_target="tpu_custom_call" | custom-call | flops 10000000 | bytes 30000000 | tf_op jit(solution)/shard_map/sum_over_dp/pallas_call | solution.py:739
  732.0 1.8 slice.16
  733.9 6.9 convert_bitcast_fusion
  740.8 1.4 fusion
  742.2 2.5 bitcast_convert_fusion
  744.7 9.7 %copy.15 = f32[768,4,768]{0,2,1:T(8,128)} copy(f32[768,4,768]{2,0,1:T(8,128)} %convert_bitcast_fusion) | data formatting | bytes 18874368 | tf_op jit(solution)/shard_map/convert_element_type | solution.py:775
  754.4 0.0 copy-start.1
  754.4 9.7 %copy.16 = f32[1,768,3072]{2,1,0:T(8,128)} copy(f32[1,768,3072]{1,2,0:T(8,128)} %bitcast.15) | data formatting | bytes 18874368
  764.1 0.0 copy-start
  764.1 0.0 copy-done.1
  764.1 1.4 copy.19
  765.5 1.1 copy-done
  766.6 1.4 copy.20
  (1 shorter events, 0.0 us)
Async XLA Ops:
  184.0 1.2 collective-permute-start
  754.4 9.7 %copy-start.1 = (bf16[3,512,768]{2,1,0:T(8,128)(2,1)S(1)}, bf16[3,512,768]{2,1,0:T(8,128)(2,1)}, u32[]{:S(2)}) copy-start(bf16[3,512,768]{2,1,0:T(8,128)(2,1)} %get-tuple-element.13) | copy-start | bytes 7077892
  764.1 2.5 copy-start

commit v2 on v1

--- a/solution.py
+++ b/solution.py
@@ -540,16 +540,18 @@
     )(tokens, cotangent, lengths, weights, w_down, vec)
 
 
-CLASS_ROWS = (112, 112, 160)
-CLASS_AT = (0, 112, 224)
-STEP_ROWS = 384
-LAG = 4
-
-
-def sum_kernel(line, g_ref, small_in, fin_ref, small_out, G, RV, FIN, SR, sem_in, sem_out, s_up, s_down, r_up, r_fin, t_up, t_down, q_up, q_fin):
+CLASS_ROWS = 48
+CLASSES = 4
+STEP_ROWS = CLASSES * CLASS_ROWS
+
+
+def sum_kernel(
+    line, g_ref, small_in, main_ref, half_ref, small_out, G, RV, FIN, SR,
+    sem_in, sem_out, s_up, s_down, r_up, r_fin, t_up, t_down, q_up, q_fin,
+):
     blocks, D, _ = g_ref.shape
-    steps = blocks * D // STEP_ROWS
     per = D // STEP_ROWS
+    steps = blocks * per
     dp = lax.axis_index("dp")
     s = lax.axis_index("section")
     y = lax.rem(dp, 2)
@@ -564,8 +566,15 @@
     def load(b):
         return pltpu.make_async_copy(g_ref.at[b], G.at[b], sem_in.at[b])
 
-    def store(b):
-        return pltpu.make_async_copy(FIN.at[b], fin_ref.at[b], sem_out.at[b])
+    def store_main(b):
+        return pltpu.make_async_copy(
+            FIN.at[b], main_ref.at[:, pl.ds(pl.multiple_of(b * D, D), D)], sem_out.at[b]
+        )
+
+    def store_half(b):
+        return pltpu.make_async_copy(
+            FIN.at[b], half_ref.at[pl.ds(pl.multiple_of((b - 4) * D, D), D)], sem_out.at[b]
+        )
 
     for b in range(blocks):
         load(b).start()
@@ -583,23 +592,26 @@
 
     pl.semaphore_wait(barrier, 1 + has_dn.astype(jnp.int32) + has_up.astype(jnp.int32))
 
-    def roles(kind, k):
+    low_mid, high_mid = line // 2 - 1, line // 2
+
+    def roles(kind):
+        root_y = kind % 2
+        k = (low_mid, high_mid)[root_y]
+        away = jnp.abs(z - k) + (y != root_y).astype(jnp.int32)
+        deep = max(k, line - 1 - k) + 1
         if kind < 2:
-            rail = y == kind
+            rail = y == root_y
             return (
                 (rail, rail & (z <= k) & has_dn, rail & (z >= k) & has_up),
                 (jnp.logical_not(rail), rail & (z > k), rail & (z < k)),
+                away, deep,
             )
         at = z == k
         return (
-            (at & (y == 0), (z <= k) & has_dn, (z >= k) & has_up),
-            (at & (y == 1), z > k, z < k),
+            (at & (y == root_y), (z <= k) & has_dn, (z >= k) & has_up),
+            (at & (y != root_y), z > k, z < k),
+            away, deep,
         )
-
-    def root_of(kind, i):
-        if kind < 2:
-            return line // 2 - 1 + lax.rem(i, 2)
-        return lax.rem(line // 2 - 1 + i, line)
 
     def rem_copy(src, dst, send, recv, dev):
         return pltpu.make_async_remote_copy(
@@ -609,31 +621,15 @@
     slot_at_parent = (0, 2, 1)
 
     def tree(kids, parents, acc, slots, fin, sup, sdown, rup, rfin):
-        def add_children():
-            for n in range(3):
-                @pl.when(kids[n])
-                def _():
-                    rem_copy(slots(n), slots(n), sup, rup(n), peers[n]).wait_recv()
-                    acc[...] = (acc[...].astype(F32) + slots(n)[...].astype(F32)).astype(acc.dtype)
+        root = jnp.logical_not(parents[0] | parents[1] | parents[2])
 
         def send_up(wait):
             for n in range(3):
                 @pl.when(parents[n])
                 def _():
-                    c = rem_copy(acc, slots(slot_at_parent[n]), sup, rup(slot_at_parent[n]), peers[n])
+                    m = slot_at_parent[n]
+                    c = rem_copy(acc, slots(m), sup, rup(m), peers[n])
                     c.wait_send() if wait else c.start()
-
-        root = jnp.logical_not(parents[0] | parents[1] | parents[2])
-
-        def finish_root():
-            @pl.when(root)
-            def _():
-                fin[...] = acc[...]
-
-        def wait_final():
-            @pl.when(jnp.logical_not(root))
-            def _():
-                rem_copy(acc, fin, sup, rfin, peers[0]).wait_recv()
 
         def send_down(wait):
             for n in range(3):
@@ -642,91 +638,98 @@
                     c = rem_copy(fin, fin, sdown(n), rfin, peers[n])
                     c.wait_send() if wait else c.start()
 
-        return root, add_children, send_up, finish_root, wait_final, send_down
+        def up():
+            for n in range(3):
+                @pl.when(kids[n])
+                def _():
+                    rem_copy(slots(n), slots(n), sup, rup(n), peers[n]).wait_recv()
+                    acc[...] = (acc[...].astype(F32) + slots(n)[...].astype(F32)).astype(acc.dtype)
+            send_up(False)
+
+            @pl.when(root)
+            def _():
+                fin[...] = acc[...]
+                send_down(False)
+
+        def down():
+            @pl.when(jnp.logical_not(root))
+            def _():
+                rem_copy(acc, fin, sup, rfin, peers[0]).wait_recv()
+                send_down(False)
+
+        def drain():
+            send_up(True)
+            send_down(True)
+
+        return up, down, drain
 
     def chunk(kind, i):
         b = i // per
-        at = pl.multiple_of(lax.rem(i, per) * STEP_ROWS + CLASS_AT[kind], 16)
-        r = pl.ds(at, CLASS_ROWS[kind])
-        kids, parents = roles(kind, root_of(kind, i))
+        r = pl.ds(pl.multiple_of(lax.rem(i, per) * STEP_ROWS + kind * CLASS_ROWS, 16), CLASS_ROWS)
+        kids, parents, _, _ = roles(kind)
         return tree(
             kids, parents, G.at[b, r], lambda n: RV.at[n, b, r], FIN.at[b, r],
             s_up.at[kind, i], lambda n: s_down.at[kind, n, i], lambda n: r_up.at[kind, n, i], r_fin.at[kind, i],
         )
 
-    def up(i):
-        @pl.when(lax.rem(i, per) == 0)
-        def _():
-            load(i // per).wait()
-
-        for kind in range(3):
-            root, add_children, send_up, finish_root, wait_final, send_down = chunk(kind, i)
-            add_children()
-            send_up(False)
-            finish_root()
-
-            @pl.when(root)
-            def _():
-                send_down(False)
-
-    def down(i):
-        for kind in range(3):
-            root, add_children, send_up, finish_root, wait_final, send_down = chunk(kind, i)
-            wait_final()
-
-            @pl.when(jnp.logical_not(root))
-            def _():
-                send_down(False)
-
-        @pl.when(lax.rem(i, per) == per - 1)
-        def _():
-            store(i // per).start()
-
     SR[3] = small_in[...]
-    kids, parents = roles(0, line // 2)
+    kids, parents, _, _ = roles(0)
     little = tree(
         kids, parents, SR.at[3], lambda n: SR.at[n], SR.at[4], t_up, lambda n: t_down.at[n], lambda n: q_up.at[n], q_fin
     )
+    little[0]()
+    deepest = max(roles(kind)[3] for kind in range(CLASSES))
+
+    def step(t, c):
+        @pl.when((lax.rem(t, per) == 0) & (t < steps))
+        def _():
+            load(t // per).wait()
+
+        for kind in range(CLASSES):
+            _, _, away, deep = roles(kind)
+            i = t - (deep - away)
+
+            @pl.when((i >= 0) & (i < steps))
+            def _():
+                chunk(kind, i)[0]()
+
+        for kind in range(CLASSES):
+            _, _, away, deep = roles(kind)
+            i = t - deep - away
+
+            @pl.when((i >= 0) & (i < steps))
+            def _():
+                chunk(kind, i)[1]()
+
+        i = t - 2 * deepest
+
+        @pl.when((i >= 0) & (lax.rem(i, per) == per - 1))
+        def _():
+            b = i // per
+
+            @pl.when(b < 4)
+            def _():
+                store_main(b).start()
+
+            @pl.when(b >= 4)
+            def _():
+                store_half(b).start()
+
+        return c
+
+    lax.fori_loop(0, steps + 2 * deepest, step, 0)
     little[1]()
-    little[2](False)
-    little[3]()
-
-    @pl.when(little[0])
-    def _():
-        little[5](False)
-
-    def step(i, c):
-        @pl.when(i < steps)
-        def _():
-            up(i)
-
-        @pl.when(i >= LAG)
-        def _():
-            down(i - LAG)
-
+    small_out[...] = SR[4]
+
+    def drain(i, c):
+        for kind in range(CLASSES):
+            chunk(kind, i)[2]()
         return c
 
-    lax.fori_loop(0, steps + LAG, step, 0)
-    little[4]()
-
-    @pl.when(jnp.logical_not(little[0]))
-    def _():
-        little[5](False)
-
-    small_out[...] = SR[4]
-
-    def drain(i, c):
-        for kind in range(3):
-            t = chunk(kind, i)
-            t[2](True)
-            t[5](True)
-        return c
-
     lax.fori_loop(0, steps, drain, 0)
-    little[2](True)
-    little[5](True)
+    little[2]()
     for b in range(blocks):
-        store(b).wait()
+        (store_main(b) if b < 4 else store_half(b)).wait()
 
 
 def sum_over_dp(grads, small):
@@ -740,18 +743,19 @@
         partial(sum_kernel, line),
         name="sum_over_dp",
         out_shape=(
-            jax.ShapeDtypeStruct(grads.shape, BF),
+            jax.ShapeDtypeStruct((D, 4 * D), BF),
+            jax.ShapeDtypeStruct((2 * D, D), BF),
             jax.ShapeDtypeStruct(small.shape, F32),
         ),
         in_specs=[any_spec, vmem_spec],
-        out_specs=(any_spec, vmem_spec),
+        out_specs=(any_spec, any_spec, vmem_spec),
         scratch_shapes=[
             pltpu.VMEM((blocks, D, D), BF),
             pltpu.VMEM((3, blocks, D, D), BF),
             pltpu.VMEM((blocks, D, D), BF),
             pltpu.VMEM((5,) + small.shape, F32),
             dma((blocks,)), dma((blocks,)),
-            dma((3, steps)), dma((3, 3, steps)), dma((3, 3, steps)), dma((3, steps)),
+            dma((CLASSES, steps)), dma((CLASSES, 3, steps)), dma((CLASSES, 3, steps)), dma((CLASSES, steps)),
             dma, dma((3,)), dma((3,)), dma,
         ],
         compiler_params=pltpu.CompilerParams(
@@ -771,9 +775,8 @@
     theirs = lax.dynamic_index_in_dim(small, 1 - p, 0, keepdims=False)
     pairs = [(i, i + 1 - 2 * (i % 2)) for i in range(lax.axis_size("section"))]
     small = mine + lax.ppermute(theirs, "section", pairs)
-    total, small = sum_over_dp(grads, small)
-    grad_main = jnp.swapaxes(total[:4], 0, 1).reshape(D, 4 * D).astype(F32)
-    grad_half = total[4:].reshape(2 * D, D).astype(F32)
+    grad_main, grad_half, small = sum_over_dp(grads, small)
+    grad_main, grad_half = grad_main.astype(F32), grad_half.astype(F32)
     return (
         kept_out[None],
         kept_grad[None],

time: 776 us -> 354 us (0.46); the launches traced: 768 us -> 354 us
  Pallas kernels: 727 us -> 333 us
  local copies, waits for them, and re-layouts: 27.4 us -> 6.2 us
    pallas_call x1, Pallas kernels: 545 us -> 152 us  [sum_over_dp(): pl.pallas_call(partial(sum_kernel, line), name='sum_over_dp', out_shape=(...]
    broadcast_in_dim x0 -> x2, other arithmetic: none -> 10.1 us  [the longest x1 7.52 us: on_device(): grad_main[None]]
    unnamed x7 -> x8, local copies, waits for them, and re-layouts: 13.7 us -> 3.93 us
    convert_element_type x1 -> x0, local copies, waits for them, and re-layouts: 9.65 us -> none  [on_device(): grad_main = jnp.swapaxes(total[:4], 0, 1).reshape(D, 4 * D).astype(F32)]
    convert_element_type x2 -> x0, other arithmetic: 9.44 us -> none  [the longest x1 6.9 us: on_device(): grad_main = jnp.swapaxes(total[:4], 0, 1).reshape(D, 4 * D).astype(F32)]
where the time goes in v2:
time: 354 us
  Pallas kernels  333 us (94%)
  other arithmetic  12.8 us (4%)
  local copies, waits for them, and re-layouts  6.2 us (2%)
    pallas_call x1, Pallas kernels, run_layers(): pl.pallas_call(layer_kernel, name='layers', out_shape=(jax.ShapeDtypeStru...  181 us
    pallas_call x1, Pallas kernels, sum_over_dp(): pl.pallas_call(partial(sum_kernel, line), name='sum_over_dp', out_shape=(...  152 us
    broadcast_in_dim x1, other arithmetic, on_device(): grad_main[None]  7.52 us
  transfers between devices with their start and end apart: 1, of which 1 were waited for; matrix products, arithmetic and copies ran while one was open for 0% of the time, Pallas kernels for 0%

profile of v2, /device:TPU:4, one launch (start us, length us, event | category | flops | bytes accessed | tf_op | source)
XLA Modules:
  0.0 353.9 jit_solution(7689117366744273467)
XLA Ops:
  0.6 0.1 pad.3.clone
  0.7 1.4 maximum_maximum_fusion.vec
  2.1 181.2 %layers.1 = (bf16[3,512,768]{2,1,0:T(8,128)(2,1)}, bf16[3,512,768]{2,1,0:T(8,128)(2,1)}, bf16[6,768,768]{2,1,0:T(8,128)(2,1)}, f32[2,8,768]{2,1,0:T(8,128)}) custom-call(bf16[3,512,768]{2,1,0:T(8,128)(2,1)} %tok.1, bf16[3,512,768]{2,1,0:T(8,128)(2,1)} %cot.1, s32[3]{0:T(128)} %lens.1, bf16[768,3072]{1,0:T(8,128)(2,1)} %bitcast.16, ...), custom_call_target="tpu_custom_call" | custom-call | flops 60000002048 | bytes 40000000 | tf_op jit(solution)/shard_map/layers/pallas_call | solution.py:498
  183.3 0.7 dynamic-slice_bitcast_fusion
  184.0 0.1 collective-permute-start
  184.1 1.1 collective-permute-done
  185.2 1.4 bitcast_add_fusion.small_in
  186.6 151.8 %sum_over_dp.1 = (bf16[768,3072]{1,0:T(8,128)(2,1)}, bf16[1536,768]{1,0:T(8,128)(2,1)}, f32[8,768]{1,0:T(8,128)}) custom-call(bf16[6,768,768]{2,1,0:T(8,128)(2,1)} %get-tuple-element.16.g_ref, f32[8,768]{1,0:T(8,128)} %bitcast_add_fusion.small_in), custom_call_target="tpu_custom_call" | custom-call | flops 10000000 | bytes 30000000 | tf_op jit(solution)/shard_map/sum_over_dp/pallas_call | solution.py:742
  338.4 1.4 fusion
  339.9 0.0 copy-start
  339.9 7.5 %bitcast_convert_fusion = f32[1,768,3072]{2,1,0:T(8,128)} fusion(bf16[768,3072]{1,0:T(8,128)(2,1)} %get-tuple-element.18), kind=kLoop, calls=%fused_computation | loop fusion | flops 2359296 | bytes 14155776 | tf_op jit(solution)/shard_map/broadcast_in_dim | solution.py:783
  347.4 0.0 copy-done
  347.4 0.0 copy-start.2
  347.4 2.5 bitcast_convert_fusion.1
  349.9 0.0 copy-done.2
  349.9 0.0 copy-start.1
  349.9 1.4 copy.17
  351.3 1.1 copy-done.1
  352.4 1.4 copy.18
  (1 shorter events, 0.0 us)
Async XLA Ops:
  184.0 1.2 collective-permute-start
  339.9 7.5 %copy-start = (bf16[1536,768]{1,0:T(8,128)(2,1)S(1)}, bf16[1536,768]{1,0:T(8,128)(2,1)}, u32[]{:S(2)}) copy-start(bf16[1536,768]{1,0:T(8,128)(2,1)} %get-tuple-element.19) | copy-start | bytes 7077892
  347.4 2.5 copy-start.2
  349.9 2.5 copy-start.1

commit v3 on v2

--- a/solution.py
+++ b/solution.py
@@ -17,7 +17,7 @@
 NN = (((1,), (0,)), ((), ()))
 NT = (((1,), (1,)), ((), ()))
 TN = (((0,), (0,)), ((), ()))
-LN_ROWS = 64
+LN_ROWS = 128
 W_ORDER = (1, 2, 0, 3)
 
 
@@ -26,19 +26,14 @@
 
 
 def gelu_pair(x):
-    ax = jnp.abs(x)
-    t = 1.0 / (1.0 + ax * (0.3275911 * 0.7071067811865476))
-    e = jnp.exp(x * x * -0.5)
-    poly = ((((0.5 * 1.061405429) * t + (0.5 * -1.453152027)) * t + (0.5 * 1.421413741)) * t + (0.5 * -0.284496736)) * t + (0.5 * 0.254829592)
-    tail = poly * t * e
-    cdf = jnp.where(x >= 0.0, 1.0 - tail, tail)
-    return x * cdf, cdf + x * (e * 0.3989422804014327)
+    cdf = 0.5 * (1.0 + lax.erf(x * 0.7071067811865476))
+    return x * cdf, cdf + x * (jnp.exp(x * x * -0.5) * 0.3989422804014327)
 
 
 def layer_kernel(
     tok, cot, lens, wm, wd, vec,
     out_ref, ing_ref, g_ref, small_ref,
-    W, W2, V, L, R, Q, KV, N, RS, LSE, H2, GIN, GMID, GOUT, RES, DCTX, DKV, DKVR, GR, GS, VR,
+    W, W2, V, L, R, KV, N, RS, LSE, GIN, GOUT, RES, DCTX, DKV, DKVR, GR, GS, VR,
     sem_w, sem_tok, sem_cot, send_w, recv_w, send_kv, recv_kv, send_h, recv_h, sem_o, recv_o,
     send_dkv, recv_dkv, send_g, recv_g, sem_i, recv_i, send_gr, recv_gr, sem_go, send_v, recv_v,
 ):
@@ -127,14 +122,14 @@
                 wd.at[pl.ds(b * D, D), :], W2.at[2 * (1 - p) + b], send_w.at[4 + b], recv_w.at[4 + b], partner
             ).wait_recv()
 
-    def send_keys(q):
-        return remote(KV.at[q, own], KV.at[q, own], send_kv.at[q], recv_kv.at[q], partner)
-
-    def take_keys(q):
-        return remote(KV.at[q, other], KV.at[q, other], send_kv.at[q], recv_kv.at[q], partner)
+    def send_keys(q, i):
+        return remote(KV.at[q, i, own], KV.at[q, i, own], send_kv.at[q, i], recv_kv.at[q, i], partner)
+
+    def take_keys(q, i):
+        return remote(KV.at[q, i, other], KV.at[q, i, other], send_kv.at[q, i], recv_kv.at[q, i], partner)
 
     def hand_on(q):
-        return remote(H2.at[q], L.at[0, rows(q)], send_h.at[q], recv_h.at[q], across)
+        return remote(GOUT.at[q], L.at[0, rows(q)], send_h.at[q], recv_h.at[q], across)
 
     def hand_back(q):
         return remote(GOUT.at[q], GIN.at[q], send_g.at[q], recv_g.at[q], across)
@@ -171,11 +166,14 @@
     low_lanes = (lane < HEAD).astype(F32)
     high_lanes = 1.0 - low_lanes
 
-    def split_lanes(x):
+    def stack_heads(x):
         wide = x.astype(F32)
-        return (wide * low_lanes).astype(BF), (wide * high_lanes).astype(BF)
-
-    key_row = lax.broadcasted_iota(jnp.int32, (seq_len, half), 0)
+        return jnp.concatenate([(wide * low_lanes).astype(BF), (wide * high_lanes).astype(BF)], axis=0)
+
+    def join_heads(x):
+        return jnp.where(lane < HEAD, x[:half], x[half:])
+
+    key_at = lax.broadcasted_iota(jnp.int32, (1, seq_len), 1)
 
     def norm_forward(sec, h_ref_at, dst, q):
         bias, gain, shift = V[sec, 0:1, :], V[sec, 1:2, :], V[sec, 2:3, :]
@@ -242,41 +240,37 @@
             need_w(0, 1)
 
         h = L[0, rows(q), :]
-        KV[q, own, 0:D] = mm(h, W[0, 1]).astype(BF)
+        KV[q, 0, own, :] = mm(h, W[0, 1]).astype(BF)
+        send_keys(q, 0).start()
 
         @pl.when(q == 0)
         def _():
             need_w(0, 2)
 
-        KV[q, own, D : 2 * D] = mm(h, W[0, 2]).astype(BF)
-        send_keys(q).start()
+        KV[q, 1, own, :] = mm(h, W[0, 2]).astype(BF)
+        send_keys(q, 1).start()
 
         @pl.when(q == 0)
         def _():
             need_w(0, 0)
 
-        Q[rows(q), :] = (mm(h, W[0, 0]) * HEAD ** (-0.5)).astype(BF)
-        take_keys(q).wait_recv()
-        valid = key_row < length
-
-        def heads(hp, c):
-            cols = pl.ds(pl.multiple_of(hp * 128, 128), 128)
-            vcols = pl.ds(pl.multiple_of(D + hp * 128, 128), 128)
-            kp = KV[q, :, cols]
-            v_t = jnp.transpose(KV[q, :, vcols])
-            done = []
-            for i, qh in enumerate(split_lanes(Q[rows(q), cols])):
-                st = jnp.where(valid, mm(kp, qh, NT), MASK_FILL)
-                top = jnp.max(st, axis=0, keepdims=True)
-                e = jnp.exp(st - top)
-                total = jnp.sum(e, axis=0, keepdims=True)
-                LSE[q, 2 * hp + i] = top + jnp.log(total)
-                ct = mm(v_t[i * HEAD : (i + 1) * HEAD, :], e.astype(BF))
-                done.append(ct * (1.0 / total))
-            L[1, rows(q), cols] = jnp.transpose(jnp.concatenate(done, axis=0)).astype(BF)
-            return c
-
-        lax.fori_loop(0, pairs, heads, 0)
+        R[0, rows(q), :] = (mm(h, W[0, 0]) * HEAD ** (-0.5)).astype(BF)
+        take_keys(q, 0).wait_recv()
+        take_keys(q, 1).wait_recv()
+        valid = key_at < length
+
+        for hp in range(pairs):
+            cols = slice(hp * 128, (hp + 1) * 128)
+            st = mm(stack_heads(R[0, rows(q), cols]), KV[q, 0, :, cols], NT)
+            st = jnp.where(valid, st, MASK_FILL)
+            top = jnp.max(st, axis=1, keepdims=True)
+            e = jnp.exp(st - top)
+            total = jnp.sum(e, axis=1, keepdims=True)
+            ct = mm(e.astype(BF), KV[q, 1, :, cols]) * (1.0 / total)
+            L[1, rows(q), cols] = join_heads(ct).astype(BF)
+            lse = top + jnp.log(total)
+            LSE[q, :, 2 * hp : 2 * hp + 1] = lse[:half]
+            LSE[q, :, 2 * hp + 1 : 2 * hp + 2] = lse[half:]
 
         @pl.when(q == 0)
         def _():
@@ -303,17 +297,15 @@
         norm_forward(0, 0, keep_mid, q)
         put_start(L.at[2, rows(q)], out_ref, q, 0, sem_o, recv_o)
 
-        def up(b, c):
-            for j in range(4):
-                @pl.when((q == 0) & (b == j))
-                def _():
-                    need_w(1, j)
+        @pl.when(q == 0)
+        def _():
+            for b in range(4):
+                need_w(1, b)
+
+        for b in range(4):
             hidden, slope = gelu_pair(mm(L[2, rows(q), :], W[1, b]))
             L[3 + b, rows(q), :] = hidden.astype(BF)
             R[5 + b, rows(q), :] = slope.astype(BF)
-            return c
-
-        lax.fori_loop(0, 4, up, 0)
 
         @pl.when(q == 0)
         def _():
@@ -327,7 +319,7 @@
             RES[:, c] = acc
 
         def keep_out(r, rq, x):
-            H2[q, r, :] = x
+            GOUT[q, r, :] = x
 
         norm_forward(1, 2, keep_out, q)
 
@@ -335,13 +327,14 @@
         def _():
             hand_on(q).start()
 
-        put_start(H2.at[q], out_ref, q, 1, sem_o, recv_o)
+        put_start(GOUT.at[q], out_ref, q, 1, sem_o, recv_o)
         return carry
 
     lax.fori_loop(0, nq, forward, 0)
 
     def send_dkeys(q):
-        return remote(DKV.at[1 - p], DKVR.at[q], send_dkv.at[q], recv_dkv.at[q], partner)
+        slot = lax.rem(q, 2)
+        return remote(DKV.at[1 - p], DKVR.at[slot], send_dkv, recv_dkv.at[slot], partner)
 
     def backward(q, carry):
         length = lens[q]
@@ -356,67 +349,63 @@
 
         norm_backward(1, GIN, 4, q)
 
-        def down(b, c):
+        for b in range(4):
             dh = mm(R[4, rows(q), :], W2[b], NT)
             R[5 + b, rows(q), :] = (dh * R[5 + b, rows(q), :].astype(F32)).astype(BF)
-            return c
-
-        lax.fori_loop(0, 4, down, 0)
 
         for n in range(D // 256):
             c = slice(n * 256, (n + 1) * 256)
             acc = RES[:, c]
             for b in range(4):
                 acc += mm(R[5 + b, rows(q), :], W[1, b, c, :], NT)
-            GMID[q, :, c] = acc.astype(BF)
-        put_start(GMID.at[q], ing_ref, q, 1, sem_i, recv_i)
-
-        norm_backward(0, GMID, 3, q)
+            GIN[q, :, c] = acc.astype(BF)
+        put_start(GIN.at[q], ing_ref, q, 1, sem_i, recv_i)
+
+        norm_backward(0, GIN, 3, q)
         DCTX[...] = mm(R[3, rows(q), :], W[0, 3], NT).astype(BF)
 
         @pl.when(q > 0)
         def _():
             send_dkeys(q - 1).wait_send()
 
-        valid = key_row < length
-
-        def heads(hp, c):
-            cols = pl.ds(pl.multiple_of(hp * 128, 128), 128)
-            vcols = pl.ds(pl.multiple_of(D + hp * 128, 128), 128)
-            kp = KV[q, :, cols]
-            vp = KV[q, :, vcols]
-            qp = Q[rows(q), cols]
-            dcp = DCTX[:, cols]
-            k_t = jnp.transpose(kp)
-            dqs, dks, dvs = [], [], []
-            for i, (qh, dch) in enumerate(zip(split_lanes(qp), split_lanes(dcp))):
-                st = jnp.where(valid, mm(kp, qh, NT), MASK_FILL)
-                prob = jnp.exp(st - LSE[q, 2 * hp + i])
-                dprob = mm(vp, dch, NT)
-                mean = jnp.sum(prob * dprob, axis=0, keepdims=True)
-                ds = (prob * (dprob - mean)).astype(BF)
-                dvs.append(mm(prob.astype(BF), dcp))
-                dks.append(mm(ds, qp))
-                dqs.append(mm(k_t[i * HEAD : (i + 1) * HEAD, :], ds))
-            dq = jnp.concatenate(dqs, axis=0) * HEAD ** (-0.5)
-            R[0, rows(q), cols] = jnp.transpose(dq).astype(BF)
-            low = lane < HEAD
-            dk = jnp.where(low, dks[0], dks[1]).astype(BF)
-            dv = jnp.where(low, dvs[0], dvs[1]).astype(BF)
-            DKV[0, :, cols] = dk[:half]
-            DKV[1, :, cols] = dk[half:]
-            DKV[0, :, vcols] = dv[:half]
-            DKV[1, :, vcols] = dv[half:]
-            return c
-
-        lax.fori_loop(0, pairs, heads, 0)
+        valid = key_at < length
+
+        for hp in range(pairs):
+            cols = slice(hp * 128, (hp + 1) * 128)
+            kp = KV[q, 0, :, cols]
+            qs = stack_heads(R[0, rows(q), cols])
+            dcs = stack_heads(DCTX[:, cols])
+            st = jnp.where(valid, mm(qs, kp, NT), MASK_FILL)
+            lse = jnp.concatenate(
+                [LSE[q, :, 2 * hp : 2 * hp + 1], LSE[q, :, 2 * hp + 1 : 2 * hp + 2]], axis=0
+            )
+            prob = jnp.exp(st - lse)
+            dprob = mm(dcs, KV[q, 1, :, cols], NT)
+            mean = jnp.sum(prob * dprob, axis=1, keepdims=True)
+            ds = (prob * (dprob - mean)).astype(BF)
+            R[0, rows(q), cols] = (join_heads(mm(ds, kp)) * HEAD ** (-0.5)).astype(BF)
+            dk = jnp.transpose(mm(jnp.transpose(qs), ds)).astype(BF)
+            dv = jnp.transpose(mm(jnp.transpose(dcs), prob.astype(BF))).astype(BF)
+            DKV[0, 0, :, cols] = dk[:half]
+            DKV[1, 0, :, cols] = dk[half:]
+            DKV[0, 1, :, cols] = dv[:half]
+            DKV[1, 1, :, cols] = dv[half:]
+
         send_dkeys(q).start()
         for n in range(D // 256):
             c = slice(n * 256, (n + 1) * 256)
             RES[:, c] = RES[:, c] + mm(R[0, rows(q), :], W[0, 0, c, :], NT)
         send_dkeys(q).wait_recv()
-        R[1, rows(q), :] = (DKV[p, :, 0:D].astype(F32) + DKVR[q, :, 0:D].astype(F32)).astype(BF)
-        R[2, rows(q), :] = (DKV[p, :, D : 2 * D].astype(F32) + DKVR[q, :, D : 2 * D].astype(F32)).astype(BF)
+        slot = lax.rem(q, 2)
+        for i in range(2):
+            R[1 + i, rows(q), :] = (DKV[p, i].astype(F32) + DKVR[slot, i].astype(F32)).astype(BF)
+
+        @pl.when(first)
+        def _():
+            hand_on(q).wait_send()
+
+        put_wait(GOUT.at[q], out_ref, q, 1, sem_o, recv_o)
+        put_wait(GIN.at[q], ing_ref, q, 1, sem_i, recv_i)
         for n in range(D // 256):
             c = slice(n * 256, (n + 1) * 256)
             acc = RES[:, c]
@@ -472,19 +461,14 @@
         send_weights2(b).wait_send()
     send_dkeys(nq - 1).wait_send()
     for q in range(nq):
-        send_keys(q).wait_send()
-
-        @pl.when(first)
-        def _():
-            hand_on(q).wait_send()
+        for i in range(2):
+            send_keys(q, i).wait_send()
 
         @pl.when(last)
         def _():
             hand_back(q).wait_send()
 
         put_wait(L.at[2, rows(q)], out_ref, q, 0, sem_o, recv_o)
-        put_wait(H2.at[q], out_ref, q, 1, sem_o, recv_o)
-        put_wait(GMID.at[q], ing_ref, q, 1, sem_i, recv_i)
         put_wait(GOUT.at[q], ing_ref, q, 0, sem_i, recv_i)
 
 
@@ -512,25 +496,22 @@
             pltpu.VMEM((2, 8, D), F32),
             pltpu.VMEM((7, tall, D), BF),
             pltpu.VMEM((9, tall, D), BF),
-            pltpu.VMEM((tall, D), BF),
-            pltpu.VMEM((nq, seq_len, 2 * D), BF),
+            pltpu.VMEM((nq, 2, seq_len, D), BF),
             pltpu.VMEM((2, tall, D), BF),
             pltpu.VMEM((2, tall, 128), F32),
-            pltpu.VMEM((nq, D // HEAD, 1, half), F32),
-            pltpu.VMEM((nq, half, D), BF),
-            pltpu.VMEM((nq, half, D), BF),
+            pltpu.VMEM((nq, half, 128), F32),
             pltpu.VMEM((nq, half, D), BF),
             pltpu.VMEM((nq, half, D), BF),
             pltpu.VMEM((half, D), F32),
             pltpu.VMEM((half, D), BF),
-            pltpu.VMEM((2, half, 2 * D), BF),
-            pltpu.VMEM((nq, half, 2 * D), BF),
+            pltpu.VMEM((2, 2, half, D), BF),
+            pltpu.VMEM((2, 2, half, D), BF),
             pltpu.VMEM((6, D, D), BF),
             pltpu.VMEM((2, D, D), BF),
             pltpu.VMEM((8, D), F32),
             dma((6,)), dma((nq,)), dma((nq,)), dma((6,)), dma((6,)),
-            dma((nq,)), dma((nq,)), dma((nq,)), dma((nq,)), dma((2, nq)), dma((nq,)),
-            dma((nq,)), dma((nq,)), dma((nq,)), dma((nq,)), dma((2, nq)), dma((nq,)),
+            dma((nq, 2)), dma((nq, 2)), dma((nq,)), dma((nq,)), dma((2, nq)), dma((nq,)),
+            dma, dma((2,)), dma((nq,)), dma((nq,)), dma((2, nq)), dma((nq,)),
             dma((6,)), dma((6,)), dma((6,)), dma, dma,
         ],
         compiler_params=pltpu.CompilerParams(

time: 354 us -> 321 us (0.907)
  Pallas kernels: 333 us -> 300 us
    pallas_call x1, Pallas kernels: 181 us -> 148 us  [run_layers(): pl.pallas_call(layer_kernel, name='layers', out_shape=(jax.ShapeDtypeStru...]
where the time goes in v3:
time: 321 us; the launch traced here: 320 us
  Pallas kernels  300 us (93%)
  other arithmetic  12.8 us (4%)
  local copies, waits for them, and re-layouts  6.2 us (2%)
    pallas_call x1, Pallas kernels, sum_over_dp(): pl.pallas_call(partial(sum_kernel, line), name='sum_over_dp', out_shape=(...  152 us
    pallas_call x1, Pallas kernels, run_layers(): pl.pallas_call(layer_kernel, name='layers', out_shape=(jax.ShapeDtypeStru...  148 us
    broadcast_in_dim x1, other arithmetic, on_device(): grad_main[None]  7.52 us
  transfers between devices with their start and end apart: 1, of which 1 were waited for; matrix products, arithmetic and copies ran while one was open for 0% of the time, Pallas kernels for 0%

profile of v3, /device:TPU:4, one launch (start us, length us, event | category | flops | bytes accessed | tf_op | source)
XLA Modules:
  0.0 320.4 jit_solution(7181665746674770245)
XLA Ops:
  0.6 0.1 pad.3.clone
  0.7 1.4 maximum_maximum_fusion.vec
  2.1 147.7 %layers.1 = (bf16[3,512,768]{2,1,0:T(8,128)(2,1)}, bf16[3,512,768]{2,1,0:T(8,128)(2,1)}, bf16[6,768,768]{2,1,0:T(8,128)(2,1)}, f32[2,8,768]{2,1,0:T(8,128)}) custom-call(bf16[3,512,768]{2,1,0:T(8,128)(2,1)} %tok.1, bf16[3,512,768]{2,1,0:T(8,128)(2,1)} %cot.1, s32[3]{0:T(128)} %lens.1, bf16[768,3072]{1,0:T(8,128)(2,1)} %bitcast.16, ...), custom_call_target="tpu_custom_call" | custom-call | flops 60000002048 | bytes 40000000 | tf_op jit(solution)/shard_map/layers/pallas_call | solution.py:482
  149.8 0.7 dynamic-slice_bitcast_fusion
  150.5 0.4 collective-permute-start
  150.9 0.8 collective-permute-done
  151.7 1.3 bitcast_add_fusion.small_in
  153.1 151.9 %sum_over_dp.1 = (bf16[768,3072]{1,0:T(8,128)(2,1)}, bf16[1536,768]{1,0:T(8,128)(2,1)}, f32[8,768]{1,0:T(8,128)}) custom-call(bf16[6,768,768]{2,1,0:T(8,128)(2,1)} %get-tuple-element.16.g_ref, f32[8,768]{1,0:T(8,128)} %bitcast_add_fusion.small_in), custom_call_target="tpu_custom_call" | custom-call | flops 10000000 | bytes 30000000 | tf_op jit(solution)/shard_map/sum_over_dp/pallas_call | solution.py:723
  305.0 1.4 fusion
  306.4 0.0 copy-start
  306.4 7.5 %bitcast_convert_fusion = f32[1,768,3072]{2,1,0:T(8,128)} fusion(bf16[768,3072]{1,0:T(8,128)(2,1)} %get-tuple-element.18), kind=kLoop, calls=%fused_computation | loop fusion | flops 2359296 | bytes 14155776 | tf_op jit(solution)/shard_map/broadcast_in_dim | solution.py:764
  313.9 0.0 copy-done
  313.9 0.0 copy-start.2
  313.9 2.5 bitcast_convert_fusion.1
  316.5 0.0 copy-done.2
  316.5 0.0 copy-start.1
  316.5 1.4 copy.17
  317.9 1.1 copy-done.1
  319.0 1.4 copy.18
  (1 shorter events, 0.0 us)
Async XLA Ops:
  150.5 1.2 collective-permute-start
  306.4 7.5 %copy-start = (bf16[1536,768]{1,0:T(8,128)(2,1)S(1)}, bf16[1536,768]{1,0:T(8,128)(2,1)}, u32[]{:S(2)}) copy-start(bf16[1536,768]{1,0:T(8,128)(2,1)} %get-tuple-element.19) | copy-start | bytes 7077892
  313.9 2.5 copy-start.2
  316.5 2.5 copy-start.1

commit v4 on v3

v4 whole, which is shorter than its diff:
```python
from functools import partial

import jax
import jax.numpy as jnp
from jax import lax
from jax.experimental import pallas as pl
from jax.experimental.pallas import tpu as pltpu
from jax.sharding import PartitionSpec as P

HEAD = 64
NORM_EPS = 1e-06
MASK_FILL = -1000000000.0
MESH = pl.DeviceIdType.MESH
BF = jnp.bfloat16
F32 = jnp.float32
MIB = 1024 * 1024
NN = (((1,), (0,)), ((), ()))
NT = (((1,), (1,)), ((), ()))
TN = (((0,), (0,)), ((), ()))
LN_ROWS = 128
W_ORDER = (1, 2, 0, 3)
CLASSES = 4
CLASS_ROWS = 48
STEP_ROWS = CLASSES * CLASS_ROWS
UNITS = 7
HOP = 1
FINAL_AT = 3
FEED_PUMP = 3
PUMP = 1
FEED_AT = 0
DOWN_AT = 4


def mm(a, b, dims=NN):
    return lax.dot_general(a, b, dims, preferred_element_type=F32)


def gelu_pair(x):
    cdf = 0.5 * (1.0 + lax.erf(x * 0.7071067811865476))
    return x * cdf, cdf + x * (jnp.exp(x * x * -0.5) * 0.3989422804014327)


def layer_kernel(
    line, tok, cot, lens, wm, wd, vec,
    out_ref, ing_ref, main_ref, half_ref, small_out,
    BIG, AW, V, A, KV, N, LSE, GIN, GOUT, RES, DKV, DKVR, G, GP, VR, S, SP, SR,
    sem_w, sem_tok, sem_cot, send_w, recv_w, send_kv, recv_kv, send_h, recv_h, sem_o, recv_o,
    send_dkv, recv_dkv, send_g, recv_g, sem_i, recv_i, send_gr, recv_gr, sem_go, recv_go, send_v, recv_v,
    send_s, recv_s, s_up, s_down, r_up, r_fin, t_up, t_down, q_up, q_fin, free_sem, final_sem,
):
    nq, seq_len, D = tok.shape
    half = seq_len // 2
    pairs = D // 128
    spare = D // HEAD
    dp = lax.axis_index("dp")
    s = lax.axis_index("section")
    p = lax.rem(s, 2)
    layer = s // 2
    partner = (dp, s + 1 - 2 * p)
    across = (dp, lax.rem(s + 2, 4))
    first = layer == 0
    last = layer == 1
    wide = D // 2
    own_wide = pl.ds(pl.multiple_of(p * wide, 128), wide)
    other_wide = pl.ds(pl.multiple_of((1 - p) * wide, 128), wide)
    own = pl.ds(pl.multiple_of(p * half, half), half)
    other = pl.ds(pl.multiple_of((1 - p) * half, half), half)

    def down_rows(core, b):
        return pl.ds(pl.multiple_of((DOWN_AT + 2 * core + b) * D, 128), D)

    def main_place(sec, b):
        return AW.at[b] if sec == 0 else BIG.at[pl.ds((FEED_AT + b) * D, D)]

    def rows(q):
        return pl.ds(pl.multiple_of(q * half, half), half)

    def copy_w(sec, b):
        return pltpu.make_async_copy(wm.at[:, pl.ds(b * D, D)], main_place(sec, b), sem_w.at[b])

    def on_core(sec, act):
        pl.when(p == sec)(act)

    def copy_w2(b):
        return pltpu.make_async_copy(wd.at[pl.ds(b * D, D), :], BIG.at[down_rows(p, b)], sem_w.at[4 + b])

    def copy_tok(q):
        return pltpu.make_async_copy(tok.at[q, own], A.at[0, rows(q)], sem_tok.at[q])

    def copy_cot(q):
        return pltpu.make_async_copy(cot.at[q, own], GIN.at[q], sem_cot.at[q])

    @pl.when(first)
    def _():
        for q in range(nq):
            copy_tok(q).start()

    for b in W_ORDER:
        on_core(0, lambda: copy_w(0, b).start())
        on_core(1, lambda: copy_w(1, b).start())
    for b in range(2):
        copy_w2(b).start()

    @pl.when(last)
    def _():
        for q in range(nq):
            copy_cot(q).start()

    y = lax.rem(dp, 2)
    z = dp // 2
    has_dn = z > 0
    has_up = z < line - 1
    side = (dp + 1 - 2 * y, s)
    below = (lax.rem(dp + 2 * line - 2, 2 * line), s)
    above = (lax.rem(dp + 2, 2 * line), s)
    peers = (side, below, above)
    peer_count = 1 + has_dn.astype(jnp.int32) + has_up.astype(jnp.int32)

    def greet(sem):
        pl.semaphore_signal(sem, inc=1, device_id=side, device_id_type=MESH)

        @pl.when(has_dn)
        def _():
            pl.semaphore_signal(sem, inc=1, device_id=below, device_id_type=MESH)

        @pl.when(has_up)
        def _():
            pl.semaphore_signal(sem, inc=1, device_id=above, device_id_type=MESH)

    barrier = pltpu.get_barrier_semaphore()
    for peer in (partner, across):
        pl.semaphore_signal(barrier, inc=1, device_id=peer, device_id_type=MESH)
    greet(barrier)
    pl.semaphore_wait(barrier, 2 + peer_count)

    def remote(src, dst, send, recv, dev):
        return pltpu.make_async_remote_copy(
            src_ref=src, dst_ref=dst, send_sem=send, recv_sem=recv, device_id=dev, device_id_type=MESH
        )

    def send_weights(sec, b):
        return remote(wm.at[:, pl.ds(b * D, D)], main_place(sec, b), send_w.at[b], recv_w.at[b], partner)

    def send_weights2(b):
        return remote(wd.at[pl.ds(b * D, D), :], BIG.at[down_rows(p, b)], send_w.at[4 + b], recv_w.at[4 + b], partner)

    def send_vec():
        return remote(vec, VR, send_v, recv_v, partner)

    send_vec().start()
    for b in W_ORDER:
        on_core(0, lambda: send_weights(0, b).start())
        on_core(1, lambda: send_weights(1, b).start())
    for b in range(2):
        send_weights2(b).start()

    def need_w(sec, b):
        on_core(sec, lambda: copy_w(sec, b).wait())
        on_core(1 - sec, lambda: send_weights(sec, b).wait_recv())

    def need_w2():
        for b in range(2):
            copy_w2(b).wait()
            remote(
                wd.at[pl.ds(b * D, D), :], BIG.at[down_rows(1 - p, b)], send_w.at[4 + b], recv_w.at[4 + b], partner
            ).wait_recv()

    def send_keys(q, i):
        return remote(KV.at[q, i, own], KV.at[q, i, own], send_kv.at[q, i], recv_kv.at[q, i], partner)

    def take_keys(q, i):
        return remote(KV.at[q, i, other], KV.at[q, i, other], send_kv.at[q, i], recv_kv.at[q, i], partner)

    def hand_on(q):
        return remote(GOUT.at[q], A.at[0, rows(q)], send_h.at[q], recv_h.at[q], across)

    def hand_back(q):
        return remote(GOUT.at[q], GIN.at[q], send_g.at[q], recv_g.at[q], across)

    def put(src, dst_ref, q, sec, sems, recvs):
        keep = pltpu.make_async_copy(src, dst_ref.at[q, own], sems.at[sec, q])
        give = remote(src, dst_ref.at[q, own], sems.at[sec, q], recvs.at[q], partner)
        return keep, give

    def put_start(src, dst_ref, q, sec, sems, recvs):
        keep, give = put(src, dst_ref, q, sec, sems, recvs)

        @pl.when(p == sec)
        def _():
            keep.start()

        @pl.when(p != sec)
        def _():
            give.start()

    def put_wait(src, dst_ref, q, sec, sems, recvs):
        keep, give = put(src, dst_ref, q, sec, sems, recvs)

        @pl.when(p == sec)
        def _():
            keep.wait()
            remote(src, dst_ref.at[q, other], sems.at[sec, q], recvs.at[q], partner).wait_recv()

        @pl.when(p != sec)
        def _():
            give.wait_send()

    lane = lax.broadcasted_iota(jnp.int32, (1, 128), 1)
    low_lanes = (lane < HEAD).astype(F32)
    high_lanes = 1.0 - low_lanes

    def stack_heads(x):
        wide = x.astype(F32)
        return jnp.concatenate([(wide * low_lanes).astype(BF), (wide * high_lanes).astype(BF)], axis=0)

    def join_heads(x):
        return jnp.where(lane < HEAD, x[:half], x[half:])

    key_at = lax.broadcasted_iota(jnp.int32, (1, seq_len), 1)

    def norm_forward(sec, h_ref_at, dst, q):
        bias, gain, shift = V[sec, 0:1, :], V[sec, 1:2, :], V[sec, 2:3, :]

        def body(i, c):
            r = pl.ds(pl.multiple_of(i * LN_ROWS, LN_ROWS), LN_ROWS)
            rq = pl.ds(pl.multiple_of(q * half + i * LN_ROWS, LN_ROWS), LN_ROWS)
            residual = A[h_ref_at, rq, :].astype(F32) + (RES[r, :] + bias)
            center = jnp.mean(residual, axis=-1, keepdims=True)
            centred = residual - center
            spread = jnp.mean(centred * centred, axis=-1, keepdims=True)
            rstd = lax.rsqrt(spread + NORM_EPS)
            normed = centred * rstd
            N[sec, rq, :] = normed.astype(BF)
            LSE[q, r, spare + sec : spare + sec + 1] = rstd
            dst(r, rq, (normed * gain + shift).astype(BF))
            return c

        lax.fori_loop(0, half // LN_ROWS, body, 0)

    def norm_backward(sec, g_ref, at, q):
        gain = V[sec, 1:2, :]

        def body(i, c):
            r = pl.ds(pl.multiple_of(i * LN_ROWS, LN_ROWS), LN_ROWS)
            rq = pl.ds(pl.multiple_of(q * half + i * LN_ROWS, LN_ROWS), LN_ROWS)
            g = g_ref[q, r, :].astype(F32)
            normed = N[sec, rq, :].astype(F32)
            rstd = LSE[q, r, spare + sec : spare + sec + 1]
            gg = g * gain
            first_mean = jnp.mean(gg, axis=-1, keepdims=True)
            second_mean = jnp.mean(gg * normed, axis=-1, keepdims=True)
            dres = rstd * (gg - first_mean - normed * second_mean)
            RES[r, :] = dres
            A[at, rq, :] = dres.astype(BF)
            b, a, t = c
            return (
                b + jnp.sum(dres, axis=0, keepdims=True),
                a + jnp.sum(g * normed, axis=0, keepdims=True),
                t + jnp.sum(g, axis=0, keepdims=True),
            )

        zero = jnp.zeros((1, D), F32)
        b, a, t = lax.fori_loop(0, half // LN_ROWS, body, (zero, zero, zero))
        S[sec, 0:1, :] += b
        S[sec, 1:2, :] += a
        S[sec, 2:3, :] += t

    S[...] = jnp.zeros_like(S)

    def forward(q, carry):
        length = lens[q]

        @pl.when(first)
        def _():
            copy_tok(q).wait()

        @pl.when(last)
        def _():
            hand_on(q).wait_recv()

        @pl.when(q == 0)
        def _():
            need_w(0, 1)

        h = A[0, rows(q), :]
        KV[q, 0, own, :] = mm(h, AW[1]).astype(BF)
        send_keys(q, 0).start()

        @pl.when(q == 0)
        def _():
            need_w(0, 2)

        KV[q, 1, own, :] = mm(h, AW[2]).astype(BF)
        send_keys(q, 1).start()

        @pl.when(q == 0)
        def _():
            need_w(0, 0)

        A[12, rows(q), :] = (mm(h, AW[0]) * HEAD ** (-0.5)).astype(BF)
        take_keys(q, 0).wait_recv()
        take_keys(q, 1).wait_recv()
        valid = key_at < length

        for hp in range(pairs):
            cols = slice(hp * 128, (hp + 1) * 128)
            st = mm(stack_heads(A[12, rows(q), cols]), KV[q, 0, :, cols], NT)
            st = jnp.where(valid, st, MASK_FILL)
            top = jnp.max(st, axis=1, keepdims=True)
            e = jnp.exp(st - top)
            total = jnp.sum(e, axis=1, keepdims=True)
            ct = mm(e.astype(BF), KV[q, 1, :, cols]) * (1.0 / total)
            A[1, rows(q), cols] = join_heads(ct).astype(BF)
            lse = top + jnp.log(total)
            LSE[q, :, 2 * hp : 2 * hp + 1] = lse[:half]
            LSE[q, :, 2 * hp + 1 : 2 * hp + 2] = lse[half:]

        @pl.when(q == 0)
        def _():
            need_w(0, 3)
            send_vec().wait_recv()
            mine = vec[...]
            theirs = VR[...]

            @pl.when(p == 0)
            def _():
                V[0] = mine
                V[1] = theirs

            @pl.when(p == 1)
            def _():
                V[0] = theirs
                V[1] = mine

        RES[...] = mm(A[1, rows(q), :], AW[3])

        def keep_mid(r, rq, x):
            A[2, rq, :] = x

        norm_forward(0, 0, keep_mid, q)
        put_start(A.at[2, rows(q)], out_ref, q, 0, sem_o, recv_o)

        @pl.when(q == 0)
        def _():
            for b in range(4):
                need_w(1, b)

        for b in range(4):
            hidden, slope = gelu_pair(mm(A[2, rows(q), :], BIG[pl.ds((FEED_AT + b) * D, D), :]))
            A[3 + b, rows(q), :] = hidden.astype(BF)
            A[7 + b, rows(q), :] = slope.astype(BF)

        @pl.when(q == 0)
        def _():
            need_w2()

        for n in range(D // 256):
            c = slice(n * 256, (n + 1) * 256)
            acc = mm(A[3, rows(q), :], BIG[pl.ds((DOWN_AT + 0) * D, D), c])
            for b in range(1, 4):
                acc += mm(A[3 + b, rows(q), :], BIG[pl.ds((DOWN_AT + b) * D, D), c])
            RES[:, c] = acc

        def keep_out(r, rq, x):
            GOUT[q, r, :] = x

        norm_forward(1, 2, keep_out, q)

        @pl.when(first)
        def _():
            hand_on(q).start()

        put_start(GOUT.at[q], out_ref, q, 1, sem_o, recv_o)
        return carry

    lax.fori_loop(0, nq, forward, 0)

    per = wide // STEP_ROWS
    steps = 12 * per
    deep = line // 2 + 1
    low_mid = line // 2 - 1

    def roles(kind):
        root_y = lax.rem(kind, 2)
        k = low_mid + root_y
        at = z == k
        ours = y == root_y
        rung = kind >= 2
        along = rung | ours
        beside = at | (kind < 2)
        kids = (ours & beside, along & (z <= k) & has_dn, along & (z >= k) & has_up)
        to_side = jnp.logical_not(ours) & beside
        move = jnp.where(to_side, 1 - 2 * y, jnp.where(z > k, -2, 2))
        slot = jnp.where(to_side, 0, jnp.where(z > k, 2, 1))
        z_up = z + jnp.where(to_side, 0, jnp.where(z > k, -1, 1))
        away = jnp.abs(z - k) + 1 - ours.astype(jnp.int32)
        return k, kids, at & ours, (lax.rem(dp + move + 2 * line, 2 * line), s), slot, z_up, away

    def heap(kind, k, n, zz, i):
        spare = jnp.where((kind == 2) | (zz == low_mid), 6, 3)
        unit = jnp.where(kind < 2, n, jnp.where(zz == k, 3 + n, spare))
        flat = i * UNITS + unit
        return BIG.at[pl.ds(pl.multiple_of(flat * CLASS_ROWS, 16), CLASS_ROWS)]

    def part(kind, i):
        return G.at[i // per, pl.ds(pl.multiple_of(lax.rem(i, per) * STEP_ROWS + kind * CLASS_ROWS, 16), CLASS_ROWS)]

    def final_at(o, row, count):
        return A.at[FINAL_AT + o // 2, pl.ds(pl.multiple_of(lax.rem(o, 2) * wide + row, 16), count)]

    def final(kind, i):
        return final_at(i // per, lax.rem(i, per) * STEP_ROWS + kind * CLASS_ROWS, CLASS_ROWS)

    def send_down(kind, i, kids):
        for n in range(3):
            @pl.when(kids[n])
            def _():
                remote(final(kind, i), final(kind, i), s_down.at[kind, n], r_fin.at[kind, i], peers[n]).start()

    def up_chunk(kind, i):
        k, kids, root, parent, slot, z_up, _ = roles(kind)
        acc = part(kind, i)
        for n in range(3):
            @pl.when(kids[n])
            def _():
                got = heap(kind, k, n, z, i)
                remote(acc, got, s_up.at[kind], r_up.at[kind, n, i], peers[n]).wait_recv()
                acc[...] = (acc[...].astype(F32) + got[...].astype(F32)).astype(BF)

        @pl.when(root)
        def _():
            final(kind, i)[...] = acc[...]
            send_down(kind, i, kids)

        @pl.when(jnp.logical_not(root))
        def _():
            remote(acc, heap(kind, k, slot, z_up, i), s_up.at[kind], r_up.at[kind, slot, i], parent).start()

    def down_chunk(kind, i):
        _, kids, root, parent, _, _, _ = roles(kind)

        @pl.when(jnp.logical_not(root))
        def _():
            remote(final(kind, i), final(kind, i), s_up.at[kind], r_fin.at[kind, i], parent).wait_recv()
            send_down(kind, i, kids)

    def store(o, wait):
        owner = jnp.where((o < 4) | ((o >= 6) & (o < 8)), 1, 0)
        is_main = (o < 4) | (o >= 8)

        def place(core):
            cols = pl.ds(pl.multiple_of(lax.rem(o, 4) * D, D), D)
            main = main_ref.at[pl.ds(pl.multiple_of(core * wide, 128), wide), cols]
            down = half_ref.at[pl.ds(pl.multiple_of(lax.rem(o, 2) * D + core * wide, 128), wide)]
            return main, down

        for here, theirs, hit in zip(place(p), place(1 - p), (is_main, jnp.logical_not(is_main))):
            @pl.when(hit & (owner == p))
            def _():
                c = pltpu.make_async_copy(final_at(o, 0, wide), here, sem_go.at[o])
                if wait:
                    c.wait()
                    remote(final_at(o, 0, wide), theirs, sem_go.at[o], recv_go.at[o], partner).wait_recv()
                else:
                    c.start()

            @pl.when(hit & (owner != p))
            def _():
                c = remote(final_at(o, 0, wide), here, sem_go.at[o], recv_go.at[o], partner)
                c.wait_send() if wait else c.start()

    def sum_step(t):
        def ups(kind, c):
            i = t - HOP * (deep - roles(kind)[6])

            @pl.when((i >= 0) & (i < steps))
            def _():
                up_chunk(kind, i)

            return c

        def downs(kind, c):
            i = t - HOP * (deep + roles(kind)[6])

            @pl.when((i >= 0) & (i < steps))
            def _():
                down_chunk(kind, i)

            return c

        lax.fori_loop(0, CLASSES, ups, 0)
        lax.fori_loop(0, CLASSES, downs, 0)
        i = t - 2 * HOP * deep

        @pl.when((i >= 0) & (lax.rem(i, per) == per - 1))
        def _():
            store(i // per, False)

    def sum_steps(lo, hi):
        def one(t, c):
            sum_step(t)
            return c

        lax.fori_loop(lo, hi, one, 0)

    def pump(q, lo, hi):
        @pl.when((q == nq - 1) & first)
        def _():
            sum_steps(lo, hi)

    def stage(j):
        return DKV.at[pl.ds(pl.multiple_of(lax.rem(j, 2) * wide, 128), wide)]

    def send_grad(j):
        return remote(stage(j), GP.at[lax.rem(j, 2)], send_gr.at[lax.rem(j, 2)], recv_gr.at[lax.rem(j, 2)], partner)

    def take_grad(j):
        send_grad(j).wait_recv()
        G[j] = (G[j].astype(F32) + GP[lax.rem(j, 2)].astype(F32)).astype(BF)

    def weight_grads(lo, hi, after):
        def one(j, c):
            left = jnp.where(j < 4, 2, jnp.where(j < 8, j - 1, jnp.where(j < 11, 0, 1)))
            right = jnp.where(j < 4, 7 + j, jnp.where(j < 8, 11, j + 4))

            @pl.when(j >= lo + 2)
            def _():
                send_grad(j - 2).wait_send()

            stage(j)[...] = mm(A[left, :, other_wide], A[right], TN).astype(BF)

            @pl.when(j > lo)
            def _():
                take_grad(j - 1)

            send_grad(j).start()
            G[j] = mm(A[left, :, own_wide], A[right], TN).astype(BF)

            @pl.when(j > lo)
            def _():
                after(j - 1)

            return c

        lax.fori_loop(lo, hi, one, 0)
        take_grad(hi - 1)
        after(hi - 1)
        for j in (hi - 2, hi - 1):
            send_grad(j).wait_send()

    def feed_grads():
        greet(free_sem)

        def after(j):
            @pl.when(j == 0)
            def _():
                pl.semaphore_wait(free_sem, peer_count)

            sum_steps(FEED_PUMP * j // 8, FEED_PUMP * (j + 1) // 8)

        weight_grads(0, 8, after)
        greet(final_sem)
        pl.semaphore_wait(final_sem, peer_count)

    def send_small():
        return remote(S.at[1 - p], SP, send_s, recv_s, partner)

    def send_dkeys(q):
        slot = lax.rem(q, 2)
        theirs = pl.ds(pl.multiple_of((1 - p) * 2 * half, 128), 2 * half)
        return remote(DKV.at[theirs], DKVR.at[slot], send_dkv, recv_dkv.at[slot], partner)

    def backward(q, carry):
        length = lens[q]

        @pl.when(last)
        def _():
            copy_cot(q).wait()

        @pl.when(first)
        def _():
            hand_back(q).wait_recv()

        norm_backward(1, GIN, 11, q)

        for b in range(4):
            dh = mm(A[11, rows(q), :], BIG[pl.ds((DOWN_AT + b) * D, D), :], NT)
            A[7 + b, rows(q), :] = (dh * A[7 + b, rows(q), :].astype(F32)).astype(BF)

        for n in range(D // 256):
            c = slice(n * 256, (n + 1) * 256)
            acc = RES[:, c]
            for b in range(4):
                acc += mm(A[7 + b, rows(q), :], BIG[pl.ds((FEED_AT + b) * D + c.start, c.stop - c.start), :], NT)
            GIN[q, :, c] = acc.astype(BF)
        put_start(GIN.at[q], ing_ref, q, 1, sem_i, recv_i)

        @pl.when(q > 0)
        def _():
            send_dkeys(q - 1).wait_send()

        @pl.when((q == nq - 1) & first)
        def _():
            feed_grads()

        norm_backward(0, GIN, 15, q)

        @pl.when(q == nq - 1)
        def _():
            send_small().start()
        A[13, rows(q), :] = mm(A[15, rows(q), :], AW[3], NT).astype(BF)

        valid = key_at < length
        pump(q, FEED_PUMP + 0 * PUMP, FEED_PUMP + 1 * PUMP)

        for hp in range(pairs):
            if hp == pairs // 2:
                pump(q, FEED_PUMP + 1 * PUMP, FEED_PUMP + 2 * PUMP)
            cols = slice(hp * 128, (hp + 1) * 128)
            kp = KV[q, 0, :, cols]
            qs = stack_heads(A[12, rows(q), cols])
            dcs = stack_heads(A[13, rows(q), cols])
            st = jnp.where(valid, mm(qs, kp, NT), MASK_FILL)
            lse = jnp.concatenate(
                [LSE[q, :, 2 * hp : 2 * hp + 1], LSE[q, :, 2 * hp + 1 : 2 * hp + 2]], axis=0
            )
            prob = jnp.exp(st - lse)
            dprob = mm(dcs, KV[q, 1, :, cols], NT)
            mean = jnp.sum(prob * dprob, axis=1, keepdims=True)
            ds = (prob * (dprob - mean)).astype(BF)
            A[12, rows(q), cols] = (join_heads(mm(ds, kp)) * HEAD ** (-0.5)).astype(BF)
            dk = jnp.transpose(mm(jnp.transpose(qs), ds)).astype(BF)
            dv = jnp.transpose(mm(jnp.transpose(dcs), prob.astype(BF))).astype(BF)
            DKV[0:half, cols] = dk[:half]
            DKV[half : 2 * half, cols] = dv[:half]
            DKV[2 * half : 3 * half, cols] = dk[half:]
            DKV[3 * half : 4 * half, cols] = dv[half:]

        send_dkeys(q).start()
        pump(q, FEED_PUMP + 2 * PUMP, FEED_PUMP + 3 * PUMP)
        for n in range(D // 256):
            c = slice(n * 256, (n + 1) * 256)
            RES[:, c] = RES[:, c] + mm(A[12, rows(q), :], AW[0, c, :], NT)
        pump(q, FEED_PUMP + 3 * PUMP, FEED_PUMP + 4 * PUMP)
        send_dkeys(q).wait_recv()
        slot = lax.rem(q, 2)
        for i in range(2):
            mine = DKV[pl.ds(pl.multiple_of((2 * p + i) * half, half), half), :]
            A[13 + i, rows(q), :] = (mine.astype(F32) + DKVR[slot, i * half : (i + 1) * half].astype(F32)).astype(BF)

        @pl.when(first)
        def _():
            hand_on(q).wait_send()

        put_wait(GOUT.at[q], out_ref, q, 1, sem_o, recv_o)
        put_wait(GIN.at[q], ing_ref, q, 1, sem_i, recv_i)
        for n in range(D // 256):
            c = slice(n * 256, (n + 1) * 256)
            acc = RES[:, c]
            for b in range(1, 3):
                acc += mm(A[12 + b, rows(q), :], AW[b, c, :], NT)
            GOUT[q, :, c] = acc.astype(BF)

        @pl.when(last)
        def _():
            hand_back(q).start()

        put_start(GOUT.at[q], ing_ref, q, 0, sem_i, recv_i)
        pump(q, FEED_PUMP + 4 * PUMP, FEED_PUMP + 5 * PUMP)
        return carry

    lax.fori_loop(0, nq, backward, 0)

    send_dkeys(nq - 1).wait_send()

    @pl.when(last)
    def _():
        feed_grads()

    before = FEED_PUMP + jnp.where(first, 5 * PUMP, 0)
    weight_grads(8, 12, lambda j: sum_steps(before + (j - 8) * PUMP, before + (j - 7) * PUMP))

    send_small().wait_recv()
    SR[3] = S[p] + SP[...]
    _, kids, root, parent, slot, _, away = roles(jnp.int32(0))

    def small_down():
        for n in range(3):
            @pl.when(kids[n])
            def _():
                remote(SR.at[4], SR.at[4], t_down.at[n], q_fin, peers[n]).start()

    def small_up():
        for n in range(3):
            @pl.when(kids[n])
            def _():
                remote(SR.at[3], SR.at[n], t_up, q_up.at[n], peers[n]).wait_recv()
                SR[3] = SR[3] + SR[n]

        @pl.when(root)
        def _():
            SR[4] = SR[3]
            small_down()

        @pl.when(jnp.logical_not(root))
        def _():
            remote(SR.at[3], SR.at[slot], t_up, q_up.at[slot], parent).start()

    small_at = steps - HOP * deep

    def tail(t, c):
        sum_step(t)

        @pl.when(t == small_at + HOP * (deep - away))
        def _():
            small_up()

        @pl.when((t == small_at + HOP * (deep + away)) & jnp.logical_not(root))
        def _():
            remote(SR.at[3], SR.at[4], t_up, q_fin, parent).wait_recv()
            small_down()

        return c

    lax.fori_loop(before + 4 * PUMP, steps + 2 * HOP * deep, tail, 0)
    small_out[...] = SR[4]

    whole = G.at[pl.ds(0, 3)]
    for kind in range(CLASSES):
        _, kids_of, root_of, parent_of, _, _, _ = roles(jnp.int32(kind))

        @pl.when(jnp.logical_not(root_of))
        def _():
            remote(whole, whole, s_up.at[kind], r_fin.at[kind, 0], parent_of).wait_send()

        for n in range(3):
            @pl.when(kids_of[n])
            def _():
                remote(whole, whole, s_down.at[kind, n], r_fin.at[kind, 0], peers[n]).wait_send()

    @pl.when(jnp.logical_not(root))
    def _():
        remote(SR.at[3], SR.at[slot], t_up, q_up.at[slot], parent).wait_send()

    for n in range(3):
        @pl.when(kids[n])
        def _():
            remote(SR.at[4], SR.at[4], t_down.at[n], q_fin, peers[n]).wait_send()

    send_small().wait_send()

    for o in range(12):
        store(jnp.int32(o), True)
    send_vec().wait_send()
    for b in range(4):
        on_core(0, lambda: send_weights(0, b).wait_send())
        on_core(1, lambda: send_weights(1, b).wait_send())
    for b in range(2):
        send_weights2(b).wait_send()
    for q in range(nq):
        for i in range(2):
            send_keys(q, i).wait_send()

        @pl.when(last)
        def _():
            hand_back(q).wait_send()

        put_wait(A.at[2, rows(q)], out_ref, q, 0, sem_o, recv_o)
        put_wait(GOUT.at[q], ing_ref, q, 0, sem_i, recv_i)


def run_layers(tokens, cotangent, lengths, weights, w_down, vec):
    nq, seq_len, D = tokens.shape
    half = seq_len // 2
    tall = nq * half
    dma = pltpu.SemaphoreType.DMA
    any_spec = pl.BlockSpec(memory_space=pl.ANY)
    vmem_spec = pl.BlockSpec(memory_space=pltpu.VMEM)
    line = lax.axis_size("dp") // 2
    steps = 6 * D // STEP_ROWS
    return pl.pallas_call(
        partial(layer_kernel, line),
        name="layers",
        out_shape=(
            jax.ShapeDtypeStruct((nq, seq_len, D), BF),
            jax.ShapeDtypeStruct((nq, seq_len, D), BF),
            jax.ShapeDtypeStruct((D, 4 * D), BF),
            jax.ShapeDtypeStruct((2 * D, D), BF),
            jax.ShapeDtypeStruct((8, D), F32),
        ),
        in_specs=[any_spec, any_spec, pl.BlockSpec(memory_space=pltpu.SMEM), any_spec, any_spec, vmem_spec],
        out_specs=(any_spec, any_spec, any_spec, any_spec, vmem_spec),
        scratch_shapes=[
            pltpu.VMEM((max(8 * D, steps * UNITS * CLASS_ROWS), D), BF),
            pltpu.VMEM((4, D, D), BF),
            pltpu.VMEM((2, 8, D), F32),
            pltpu.VMEM((16, tall, D), BF),
            pltpu.VMEM((nq, 2, seq_len, D), BF),
            pltpu.VMEM((2, tall, D), BF),
            pltpu.VMEM((nq, half, 128), F32),
            pltpu.VMEM((nq, half, D), BF),
            pltpu.VMEM((nq, half, D), BF),
            pltpu.VMEM((half, D), F32),
            pltpu.VMEM((4 * half, D), BF),
            pltpu.VMEM((2, 2 * half, D), BF),
            pltpu.VMEM((12, D // 2, D), BF),
            pltpu.VMEM((2, D // 2, D), BF),
            pltpu.VMEM((8, D), F32),
            pltpu.VMEM((2, 8, D), F32),
            pltpu.VMEM((8, D), F32),
            pltpu.VMEM((5, 8, D), F32),
            dma((6,)), dma((nq,)), dma((nq,)), dma((6,)), dma((6,)),
            dma((nq, 2)), dma((nq, 2)), dma((nq,)), dma((nq,)), dma((2, nq)), dma((nq,)),
            dma, dma((2,)), dma((nq,)), dma((nq,)), dma((2, nq)), dma((nq,)),
            dma((2,)), dma((2,)), dma((12,)), dma((12,)), dma, dma,
            dma, dma, dma((CLASSES,)), dma((CLASSES, 3)), dma((CLASSES, 3, steps)), dma((CLASSES, steps)),
            dma, dma((3,)), dma((3,)), dma, pltpu.SemaphoreType.REGULAR, pltpu.SemaphoreType.REGULAR,
        ],
        compiler_params=pltpu.CompilerParams(
            collective_id=0, has_side_effects=True, vmem_limit_bytes=64 * MIB
        ),
        cost_estimate=pl.CostEstimate(flops=60 * 10**9, bytes_accessed=40 * 10**6, transcendentals=10**7),
    )(tokens, cotangent, lengths, weights, w_down, vec)


def on_device(tokens, lengths, w_main, w_down_half, out_bias, ln_gain, ln_bias, cotangent):
    D = tokens.shape[-1]
    vec = jnp.concatenate([out_bias, ln_gain, ln_bias, jnp.zeros((5, D), F32)], axis=0)
    kept_out, kept_grad, grad_main, grad_half, small = run_layers(
        tokens, cotangent, lengths, w_main[0], w_down_half[0], vec
    )
    grad_main, grad_half = grad_main.astype(F32), grad_half.astype(F32)
    return (
        kept_out[None],
        kept_grad[None],
        grad_main[None],
        grad_half[None],
        small[0:1],
        small[1:2],
        small[2:3],
    )


def solution(mesh):
    in_specs = (
        P("dp", None, None),
        P("dp"),
        P("section", None, None),
        P("section", None, None),
        P("section", None),
        P("section", None),
        P("section", None),
        P("dp", None, None),
    )
    out_specs = (
        P("section", "dp", None, None),
        P("section", "dp", None, None),
        P("section", None, None),
        P("section", None, None),
        P("section", None),
        P("section", None),
        P("section", None),
    )
    return jax.shard_map(
        on_device, mesh=mesh, in_specs=in_specs, out_specs=out_specs, check_vma=False
    )
```

time: 321 us -> 291 us (0.907); the launches traced: 320 us -> 287 us
  Pallas kernels: 300 us -> 269 us
    pallas_call x2 -> x1, Pallas kernels: 300 us -> 269 us  [run_layers(): pl.pallas_call(partial(layer_kernel, line), name='layers', out_shape=(jax...]
  transfers between devices with their start and end apart: 1 -> 0, of which waited for: 1 -> 0; matrix products, arithmetic and copies ran while one was open for 0% -> 0% of each run, Pallas kernels for 0% -> 0%
where the time goes in v4:
time: 291 us; the launch traced here: 287 us
  Pallas kernels  269 us (92%)
  other arithmetic  11.5 us (4%)
  local copies, waits for them, and re-layouts  5.45 us (2%)
    pallas_call x1, Pallas kernels, run_layers(): pl.pallas_call(partial(layer_kernel, line), name='layers', out_shape=(jax...  269 us
    broadcast_in_dim x1, other arithmetic, on_device(): grad_main[None]  7.52 us

profile of v4, /device:TPU:4, one launch (start us, length us, event | category | flops | bytes accessed | tf_op | source)
XLA Modules:
  0.0 286.9 jit_solution(1385128031111043414)
XLA Ops:
  0.6 0.1 pad.3.clone
  0.7 1.4 maximum_maximum_fusion.vec
  2.1 269.4 %layers.1 = (bf16[3,512,768]{2,1,0:T(8,128)(2,1)}, bf16[3,512,768]{2,1,0:T(8,128)(2,1)}, bf16[768,3072]{1,0:T(8,128)(2,1)}, bf16[1536,768]{1,0:T(8,128)(2,1)}, f32[8,768]{1,0:T(8,128)}) custom-call(bf16[3,512,768]{2,1,0:T(8,128)(2,1)} %tok.1, bf16[3,512,768]{2,1,0:T(8,128)(2,1)} %cot.1, s32[3]{0:T(128)} %lens.1, bf16[768,3072]{1,0:T(8,128)(2,1)} %bitcast.12, ...), custom_call_target="tpu_custom_call" | custom-call | flops 60000002048 | bytes 40000000 | tf_op jit(solution)/shard_map/layers/pallas_call | solution.py:781
  271.5 1.4 fusion
  272.9 0.0 copy-start
  272.9 7.5 %bitcast_convert_fusion = f32[1,768,3072]{2,1,0:T(8,128)} fusion(bf16[768,3072]{1,0:T(8,128)(2,1)} %get-tuple-element.14), kind=kLoop, calls=%fused_computation | loop fusion | flops 2359296 | bytes 14155776 | tf_op jit(solution)/shard_map/broadcast_in_dim | solution.py:836
  280.5 0.0 copy-done
  280.5 0.0 copy-start.2
  280.5 2.5 bitcast_convert_fusion.1
  283.0 0.0 copy-done.2
  283.0 0.0 copy-start.1
  283.0 1.4 copy.17
  284.4 1.1 copy-done.1
  285.5 1.4 copy.18
  (1 shorter events, 0.0 us)
Async XLA Ops:
  272.9 7.5 %copy-start = (bf16[1536,768]{1,0:T(8,128)(2,1)S(1)}, bf16[1536,768]{1,0:T(8,128)(2,1)}, u32[]{:S(2)}) copy-start(bf16[1536,768]{1,0:T(8,128)(2,1)} %get-tuple-element.15) | copy-start | bytes 7077892
  280.5 2.5 copy-start.2
  283.0 2.5 copy-start.1

commit v5 on v4

--- a/solution.py
+++ b/solution.py
@@ -19,6 +19,8 @@
 TN = (((0,), (0,)), ((), ()))
 LN_ROWS = 128
 W_ORDER = (1, 2, 0, 3)
+FIRST = (slice(0, 256), slice(256, 768))
+LAST = (slice(0, 512), slice(512, 768))
 CLASSES = 4
 CLASS_ROWS = 48
 STEP_ROWS = CLASSES * CLASS_ROWS
@@ -41,9 +43,9 @@
 
 
 def layer_kernel(
-    line, tok, cot, lens, wm, wd, vec,
+    line, tok, cot, lens, wm, wd, bias_in, gain_in, shift_in,
     out_ref, ing_ref, main_ref, half_ref, small_out,
-    BIG, AW, V, A, KV, N, LSE, GIN, GOUT, RES, DKV, DKVR, G, GP, VR, S, SP, SR,
+    BIG, AW, V, A, KV, N, LSE, GIN, GOUT, RES, DKV, DKVR, G, GP, S, SP, SR,
     sem_w, sem_tok, sem_cot, send_w, recv_w, send_kv, recv_kv, send_h, recv_h, sem_o, recv_o,
     send_dkv, recv_dkv, send_g, recv_g, sem_i, recv_i, send_gr, recv_gr, sem_go, recv_go, send_v, recv_v,
     send_s, recv_s, s_up, s_down, r_up, r_fin, t_up, t_down, q_up, q_fin, free_sem, final_sem,
@@ -145,14 +147,22 @@
         return remote(wd.at[pl.ds(b * D, D), :], BIG.at[down_rows(p, b)], send_w.at[4 + b], recv_w.at[4 + b], partner)
 
     def send_vec():
-        return remote(vec, VR, send_v, recv_v, partner)
-
+        return remote(V.at[p], V.at[p], send_v, recv_v, partner)
+
+    V[p] = jnp.concatenate([bias_in[...], gain_in[...], shift_in[...], jnp.zeros((5, D), F32)], axis=0)
     send_vec().start()
-    for b in W_ORDER:
+    for b in range(4):
+        on_core(1, lambda: send_weights(1, b).start())
+    for b in W_ORDER[:2]:
         on_core(0, lambda: send_weights(0, b).start())
-        on_core(1, lambda: send_weights(1, b).start())
-    for b in range(2):
-        send_weights2(b).start()
+
+    def send_later():
+        for b in W_ORDER[:2]:
+            on_core(0, lambda: send_weights(0, b).wait_send())
+        for b in W_ORDER[2:]:
+            on_core(0, lambda: send_weights(0, b).start())
+        for b in range(2):
+            send_weights2(b).start()
 
     def need_w(sec, b):
         on_core(sec, lambda: copy_w(sec, b).wait())
@@ -165,11 +175,13 @@
                 wd.at[pl.ds(b * D, D), :], BIG.at[down_rows(1 - p, b)], send_w.at[4 + b], recv_w.at[4 + b], partner
             ).wait_recv()
 
-    def send_keys(q, i):
-        return remote(KV.at[q, i, own], KV.at[q, i, own], send_kv.at[q, i], recv_kv.at[q, i], partner)
-
-    def take_keys(q, i):
-        return remote(KV.at[q, i, other], KV.at[q, i, other], send_kv.at[q, i], recv_kv.at[q, i], partner)
+    def send_keys(q, i, group):
+        here = KV.at[q, i, own, FIRST[group]]
+        return remote(here, here, send_kv.at[q, i, group], recv_kv.at[q, i, group], partner)
+
+    def take_keys(q, i, group):
+        here = KV.at[q, i, other, FIRST[group]]
+        return remote(here, here, send_kv.at[q, i, group], recv_kv.at[q, i, group], partner)
 
     def hand_on(q):
         return remote(GOUT.at[q], A.at[0, rows(q)], send_h.at[q], recv_h.at[q], across)
@@ -281,29 +293,28 @@
         @pl.when(q == 0)
         def _():
             need_w(0, 1)
+            need_w(0, 2)
 
         h = A[0, rows(q), :]
-        KV[q, 0, own, :] = mm(h, AW[1]).astype(BF)
-        send_keys(q, 0).start()
+        for group, cols in enumerate(FIRST):
+            for i in range(2):
+                KV[q, i, own, cols] = mm(h, AW[1 + i, :, cols]).astype(BF)
+                send_keys(q, i, group).start()
 
         @pl.when(q == 0)
         def _():
-            need_w(0, 2)
-
-        KV[q, 1, own, :] = mm(h, AW[2]).astype(BF)
-        send_keys(q, 1).start()
-
-        @pl.when(q == 0)
-        def _():
+            send_later()
             need_w(0, 0)
 
         A[12, rows(q), :] = (mm(h, AW[0]) * HEAD ** (-0.5)).astype(BF)
-        take_keys(q, 0).wait_recv()
-        take_keys(q, 1).wait_recv()
         valid = key_at < length
 
         for hp in range(pairs):
             cols = slice(hp * 128, (hp + 1) * 128)
+            for group in range(2):
+                if FIRST[group].start == cols.start:
+                    for i in range(2):
+                        take_keys(q, i, group).wait_recv()
             st = mm(stack_heads(A[12, rows(q), cols]), KV[q, 0, :, cols], NT)
             st = jnp.where(valid, st, MASK_FILL)
             top = jnp.max(st, axis=1, keepdims=True)
@@ -318,19 +329,7 @@
         @pl.when(q == 0)
         def _():
             need_w(0, 3)
-            send_vec().wait_recv()
-            mine = vec[...]
-            theirs = VR[...]
-
-            @pl.when(p == 0)
-            def _():
-                V[0] = mine
-                V[1] = theirs
-
-            @pl.when(p == 1)
-            def _():
-                V[0] = theirs
-                V[1] = mine
+            remote(V.at[1 - p], V.at[1 - p], send_v, recv_v, partner).wait_recv()
 
         RES[...] = mm(A[1, rows(q), :], AW[3])
 
@@ -556,7 +555,7 @@
             def _():
                 pl.semaphore_wait(free_sem, peer_count)
 
-            sum_steps(FEED_PUMP * j // 8, FEED_PUMP * (j + 1) // 8)
+            sum_steps((FEED_PUMP * j + 7) // 8, (FEED_PUMP * (j + 1) + 7) // 8)
 
         weight_grads(0, 8, after)
         greet(final_sem)
@@ -565,10 +564,13 @@
     def send_small():
         return remote(S.at[1 - p], SP, send_s, recv_s, partner)
 
-    def send_dkeys(q):
+    def send_dkeys(q, group):
         slot = lax.rem(q, 2)
         theirs = pl.ds(pl.multiple_of((1 - p) * 2 * half, 128), 2 * half)
-        return remote(DKV.at[theirs], DKVR.at[slot], send_dkv, recv_dkv.at[slot], partner)
+        return remote(
+            DKV.at[theirs, LAST[group]], DKVR.at[slot, :, LAST[group]],
+            send_dkv.at[group], recv_dkv.at[slot, group], partner,
+        )
 
     def backward(q, carry):
         length = lens[q]
@@ -597,7 +599,8 @@
 
         @pl.when(q > 0)
         def _():
-            send_dkeys(q - 1).wait_send()
+            for group in range(2):
+                send_dkeys(q - 1, group).wait_send()
 
         @pl.when((q == nq - 1) & first)
         def _():
@@ -614,7 +617,8 @@
         pump(q, FEED_PUMP + 0 * PUMP, FEED_PUMP + 1 * PUMP)
 
         for hp in range(pairs):
-            if hp == pairs // 2:
+            if LAST[1].start == hp * 128:
+                send_dkeys(q, 0).start()
                 pump(q, FEED_PUMP + 1 * PUMP, FEED_PUMP + 2 * PUMP)
             cols = slice(hp * 128, (hp + 1) * 128)
             kp = KV[q, 0, :, cols]
@@ -636,13 +640,14 @@
             DKV[2 * half : 3 * half, cols] = dk[half:]
             DKV[3 * half : 4 * half, cols] = dv[half:]
 
-        send_dkeys(q).start()
+        send_dkeys(q, 1).start()
         pump(q, FEED_PUMP + 2 * PUMP, FEED_PUMP + 3 * PUMP)
         for n in range(D // 256):
             c = slice(n * 256, (n + 1) * 256)
             RES[:, c] = RES[:, c] + mm(A[12, rows(q), :], AW[0, c, :], NT)
         pump(q, FEED_PUMP + 3 * PUMP, FEED_PUMP + 4 * PUMP)
-        send_dkeys(q).wait_recv()
+        for group in range(2):
+            send_dkeys(q, group).wait_recv()
         slot = lax.rem(q, 2)
         for i in range(2):
             mine = DKV[pl.ds(pl.multiple_of((2 * p + i) * half, half), half), :]
@@ -671,7 +676,8 @@
 
     lax.fori_loop(0, nq, backward, 0)
 
-    send_dkeys(nq - 1).wait_send()
+    for group in range(2):
+        send_dkeys(nq - 1, group).wait_send()
 
     @pl.when(last)
     def _():
@@ -753,13 +759,15 @@
         store(jnp.int32(o), True)
     send_vec().wait_send()
     for b in range(4):
+        on_core(1, lambda: send_weights(1, b).wait_send())
+    for b in W_ORDER[2:]:
         on_core(0, lambda: send_weights(0, b).wait_send())
-        on_core(1, lambda: send_weights(1, b).wait_send())
     for b in range(2):
         send_weights2(b).wait_send()
     for q in range(nq):
         for i in range(2):
-            send_keys(q, i).wait_send()
+            for group in range(2):
+                send_keys(q, i, group).wait_send()
 
         @pl.when(last)
         def _():
@@ -769,7 +777,7 @@
         put_wait(GOUT.at[q], ing_ref, q, 0, sem_i, recv_i)
 
 
-def run_layers(tokens, cotangent, lengths, weights, w_down, vec):
+def run_layers(tokens, cotangent, lengths, weights, w_down, *rows):
     nq, seq_len, D = tokens.shape
     half = seq_len // 2
     tall = nq * half
@@ -788,7 +796,7 @@
             jax.ShapeDtypeStruct((2 * D, D), BF),
             jax.ShapeDtypeStruct((8, D), F32),
         ),
-        in_specs=[any_spec, any_spec, pl.BlockSpec(memory_space=pltpu.SMEM), any_spec, any_spec, vmem_spec],
+        in_specs=[any_spec, any_spec, pl.BlockSpec(memory_space=pltpu.SMEM), any_spec, any_spec] + [vmem_spec] * 3,
         out_specs=(any_spec, any_spec, any_spec, any_spec, vmem_spec),
         scratch_shapes=[
             pltpu.VMEM((max(8 * D, steps * UNITS * CLASS_ROWS), D), BF),
@@ -805,13 +813,12 @@
             pltpu.VMEM((2, 2 * half, D), BF),
             pltpu.VMEM((12, D // 2, D), BF),
             pltpu.VMEM((2, D // 2, D), BF),
-            pltpu.VMEM((8, D), F32),
             pltpu.VMEM((2, 8, D), F32),
             pltpu.VMEM((8, D), F32),
             pltpu.VMEM((5, 8, D), F32),
             dma((6,)), dma((nq,)), dma((nq,)), dma((6,)), dma((6,)),
-            dma((nq, 2)), dma((nq, 2)), dma((nq,)), dma((nq,)), dma((2, nq)), dma((nq,)),
-            dma, dma((2,)), dma((nq,)), dma((nq,)), dma((2, nq)), dma((nq,)),
+            dma((nq, 2, 2)), dma((nq, 2, 2)), dma((nq,)), dma((nq,)), dma((2, nq)), dma((nq,)),
+            dma((2,)), dma((2, 2)), dma((nq,)), dma((nq,)), dma((2, nq)), dma((nq,)),
             dma((2,)), dma((2,)), dma((12,)), dma((12,)), dma, dma,
             dma, dma, dma((CLASSES,)), dma((CLASSES, 3)), dma((CLASSES, 3, steps)), dma((CLASSES, steps)),
             dma, dma((3,)), dma((3,)), dma, pltpu.SemaphoreType.REGULAR, pltpu.SemaphoreType.REGULAR,
@@ -820,24 +827,61 @@
             collective_id=0, has_side_effects=True, vmem_limit_bytes=64 * MIB
         ),
         cost_estimate=pl.CostEstimate(flops=60 * 10**9, bytes_accessed=40 * 10**6, transcendentals=10**7),
-    )(tokens, cotangent, lengths, weights, w_down, vec)
+    )(tokens, cotangent, lengths, weights, w_down, *rows)
+
+
+def result_kernel(out_in, grad_in, main_in, half_in, small_in, out, grad, main, down, bias, gain, shift):
+    out[...] = out_in[...]
+    grad[...] = grad_in[...]
+    main[...] = main_in[...].astype(F32)
+    down[...] = half_in[...].astype(F32)
+    bias[...] = small_in[0:1, :]
+    gain[...] = small_in[1:2, :]
+    shift[...] = small_in[2:3, :]
+
+
+RESULT_STEPS = 8
+
+
+def results(*arrays):
+    types = (BF, BF, F32, F32)
+
+    def rows_of(a):
+        return pl.BlockSpec((a.shape[0] // RESULT_STEPS, a.shape[1]), lambda i: (i, 0))
+
+    def whole(a, rows):
+        return pl.BlockSpec((rows, a.shape[1]), lambda i: (0, 0))
+
+    small = arrays[4]
+    return pl.pallas_call(
+        result_kernel,
+        name="results",
+        grid=(RESULT_STEPS,),
+        out_shape=tuple(jax.ShapeDtypeStruct(a.shape, t) for a, t in zip(arrays[:4], types))
+        + tuple(jax.ShapeDtypeStruct((1, small.shape[1]), F32) for _ in range(3)),
+        in_specs=[rows_of(a) for a in arrays[:4]] + [whole(small, 8)],
+        out_specs=tuple(rows_of(a) for a in arrays[:4]) + tuple(whole(small, 1) for _ in range(3)),
+        compiler_params=pltpu.CompilerParams(vmem_limit_bytes=63 * MIB),
+    )(*arrays)
 
 
 def on_device(tokens, lengths, w_main, w_down_half, out_bias, ln_gain, ln_bias, cotangent):
-    D = tokens.shape[-1]
-    vec = jnp.concatenate([out_bias, ln_gain, ln_bias, jnp.zeros((5, D), F32)], axis=0)
+    nq, seq_len, D = tokens.shape
     kept_out, kept_grad, grad_main, grad_half, small = run_layers(
-        tokens, cotangent, lengths, w_main[0], w_down_half[0], vec
+        tokens, cotangent, lengths, w_main[0], w_down_half[0], out_bias, ln_gain, ln_bias
     )
-    grad_main, grad_half = grad_main.astype(F32), grad_half.astype(F32)
+    tall = nq * seq_len
+    kept_out, kept_grad, grad_main, grad_half, bias, gain, shift = results(
+        kept_out.reshape(tall, D), kept_grad.reshape(tall, D), grad_main, grad_half, small
+    )
     return (
-        kept_out[None],
-        kept_grad[None],
+        kept_out.reshape(1, nq, seq_len, D),
+        kept_grad.reshape(1, nq, seq_len, D),
         grad_main[None],
         grad_half[None],
-        small[0:1],
-        small[1:2],
-        small[2:3],
+        bias,
+        gain,
+        shift,
     )
 
 

time: 291 us -> 281 us (0.966)
  other arithmetic: 11.5 us -> 0 us
  Pallas kernels: 269 us -> 277 us
  local copies, waits for them, and re-layouts: 5.45 us -> 0 us
    pallas_call x0 -> x1, Pallas kernels: none -> 11.9 us  [results(): pl.pallas_call(result_kernel, name='results', grid=(RESULT_STEPS,), out_s...]
    broadcast_in_dim x2 -> x0, other arithmetic: 10.1 us -> none  [the longest x1 7.52 us: on_device(): grad_main[None]]
    pallas_call x1, Pallas kernels: 269 us -> 265 us  [run_layers(): pl.pallas_call(partial(layer_kernel, line), name='layers', out_shape=(jax...]
    unnamed x8 -> x0, local copies, waits for them, and re-layouts: 3.93 us -> none
where the time goes in v5:
time: 281 us; the launch traced here: 278 us
  Pallas kernels  277 us (99%)
    pallas_call x1, Pallas kernels, run_layers(): pl.pallas_call(partial(layer_kernel, line), name='layers', out_shape=(jax...  265 us
    pallas_call x1, Pallas kernels, results(): pl.pallas_call(result_kernel, name='results', grid=(RESULT_STEPS,), out_s...  11.9 us

profile of v5, /device:TPU:4, one launch (start us, length us, event | category | flops | bytes accessed | tf_op | source)
XLA Modules:
  0.0 277.8 jit_solution(3006870670557485200)
XLA Ops:
  0.6 265.1 %layers.1 = (bf16[3,512,768]{2,1,0:T(8,128)(2,1)}, bf16[3,512,768]{2,1,0:T(8,128)(2,1)}, bf16[768,3072]{1,0:T(8,128)(2,1)}, bf16[1536,768]{1,0:T(8,128)(2,1)}, f32[8,768]{1,0:T(8,128)}) custom-call(bf16[3,512,768]{2,1,0:T(8,128)(2,1)} %tok.1, bf16[3,512,768]{2,1,0:T(8,128)(2,1)} %cot.1, s32[3]{0:T(128)} %lens.1, bf16[768,3072]{1,0:T(8,128)(2,1)} %bitcast.11, ...), custom_call_target="tpu_custom_call" | custom-call | flops 60000002048 | bytes 40000000 | tf_op jit(solution)/shard_map/layers/pallas_call | solution.py:789
  265.7 11.9 %results.1 = (bf16[1536,768]{1,0:T(8,128)(2,1)}, bf16[1536,768]{1,0:T(8,128)(2,1)}, f32[768,3072]{1,0:T(8,128)}, f32[1536,768]{1,0:T(8,128)}, f32[1,768]{1,0:T(1...) custom-call(bf16[1536,768]{1,0:T(8,128)(2,1)} %bitcast.8, bf16[1536,768]{1,0:T(8,128)(2,1)} %bitcast.9, ...), custom_call_target="tpu_custom_call" | custom-call | tf_op jit(solution)/shard_map/results/pallas_call | solution.py:856

commit v6 on v5

--- a/solution.py
+++ b/solution.py
@@ -25,6 +25,7 @@
 CLASS_ROWS = 48
 STEP_ROWS = CLASSES * CLASS_ROWS
 UNITS = 7
+GUEST = 10
 HOP = 1
 FINAL_AT = 3
 FEED_PUMP = 3
@@ -48,7 +49,7 @@
     BIG, AW, V, A, KV, N, LSE, GIN, GOUT, RES, DKV, DKVR, G, GP, S, SP, SR,
     sem_w, sem_tok, sem_cot, send_w, recv_w, send_kv, recv_kv, send_h, recv_h, sem_o, recv_o,
     send_dkv, recv_dkv, send_g, recv_g, sem_i, recv_i, send_gr, recv_gr, sem_go, recv_go, send_v, recv_v,
-    send_s, recv_s, s_up, s_down, r_up, r_fin, t_up, t_down, q_up, q_fin, free_sem, final_sem,
+    send_s, recv_s, s_up, s_down, r_up, r_fin, t_up, t_down, q_up, q_fin, free_sem, final_sem, send_lend, recv_lend, send_back, recv_back,
 ):
     nq, seq_len, D = tok.shape
     half = seq_len // 2
@@ -375,7 +376,8 @@
     lax.fori_loop(0, nq, forward, 0)
 
     per = wide // STEP_ROWS
-    steps = 12 * per
+    done = jnp.where(first, 11, 13)
+    steps = done * per
     deep = line // 2 + 1
     low_mid = line // 2 - 1
 
@@ -443,7 +445,17 @@
             remote(final(kind, i), final(kind, i), s_up.at[kind], r_fin.at[kind, i], parent).wait_recv()
             send_down(kind, i, kids)
 
+    def place_of(o):
+        return o + jnp.where(last & (o >= GUEST), 1, 0)
+
+    def lend():
+        return remote(G.at[11], G.at[GUEST], send_lend, recv_lend, across)
+
+    def give_back():
+        return remote(final_at(GUEST, 0, wide), final_at(11, 0, wide), send_back, recv_back, across)
+
     def store(o, wait):
+        lies = final_at(place_of(o), 0, wide)
         owner = jnp.where((o < 4) | ((o >= 6) & (o < 8)), 1, 0)
         is_main = (o < 4) | (o >= 8)
 
@@ -456,16 +468,16 @@
         for here, theirs, hit in zip(place(p), place(1 - p), (is_main, jnp.logical_not(is_main))):
             @pl.when(hit & (owner == p))
             def _():
-                c = pltpu.make_async_copy(final_at(o, 0, wide), here, sem_go.at[o])
+                c = pltpu.make_async_copy(lies, here, sem_go.at[o])
                 if wait:
                     c.wait()
-                    remote(final_at(o, 0, wide), theirs, sem_go.at[o], recv_go.at[o], partner).wait_recv()
+                    remote(lies, theirs, sem_go.at[o], recv_go.at[o], partner).wait_recv()
                 else:
                     c.start()
 
             @pl.when(hit & (owner != p))
             def _():
-                c = remote(final_at(o, 0, wide), here, sem_go.at[o], recv_go.at[o], partner)
+                c = remote(lies, here, sem_go.at[o], recv_go.at[o], partner)
                 c.wait_send() if wait else c.start()
 
     def sum_step(t):
@@ -493,7 +505,16 @@
 
         @pl.when((i >= 0) & (lax.rem(i, per) == per - 1))
         def _():
-            store(i // per, False)
+            o = i // per
+            guest = last & (o == GUEST)
+
+            @pl.when(guest)
+            def _():
+                give_back().start()
+
+            @pl.when(jnp.logical_not(guest))
+            def _():
+                store(o - jnp.where(last & (o > GUEST), 1, 0), False)
 
     def sum_steps(lo, hi):
         def one(t, c):
@@ -515,7 +536,8 @@
 
     def take_grad(j):
         send_grad(j).wait_recv()
-        G[j] = (G[j].astype(F32) + GP[lax.rem(j, 2)].astype(F32)).astype(BF)
+        o = place_of(j)
+        G[o] = (G[o].astype(F32) + GP[lax.rem(j, 2)].astype(F32)).astype(BF)
 
     def weight_grads(lo, hi, after):
         def one(j, c):
@@ -533,7 +555,7 @@
                 take_grad(j - 1)
 
             send_grad(j).start()
-            G[j] = mm(A[left, :, own_wide], A[right], TN).astype(BF)
+            G[place_of(j)] = mm(A[left, :, own_wide], A[right], TN).astype(BF)
 
             @pl.when(j > lo)
             def _():
@@ -686,6 +708,10 @@
     before = FEED_PUMP + jnp.where(first, 5 * PUMP, 0)
     weight_grads(8, 12, lambda j: sum_steps(before + (j - 8) * PUMP, before + (j - 7) * PUMP))
 
+    @pl.when(first)
+    def _():
+        lend().start()
+
     send_small().wait_recv()
     SR[3] = S[p] + SP[...]
     _, kids, root, parent, slot, _, away = roles(jnp.int32(0))
@@ -715,6 +741,10 @@
     small_at = steps - HOP * deep
 
     def tail(t, c):
+        @pl.when(last & (t == GUEST * per))
+        def _():
+            lend().wait_recv()
+
         sum_step(t)
 
         @pl.when(t == small_at + HOP * (deep - away))
@@ -731,18 +761,25 @@
     lax.fori_loop(before + 4 * PUMP, steps + 2 * HOP * deep, tail, 0)
     small_out[...] = SR[4]
 
-    whole = G.at[pl.ds(0, 3)]
+    @pl.when(first)
+    def _():
+        give_back().wait_recv()
+        store(jnp.int32(11), False)
+
+    whole_first = G.at[pl.ds(0, 11), pl.ds(0, per * CLASS_ROWS)]
+    whole_last = G.at[pl.ds(0, 13), pl.ds(0, per * CLASS_ROWS)]
     for kind in range(CLASSES):
         _, kids_of, root_of, parent_of, _, _, _ = roles(jnp.int32(kind))
 
-        @pl.when(jnp.logical_not(root_of))
-        def _():
-            remote(whole, whole, s_up.at[kind], r_fin.at[kind, 0], parent_of).wait_send()
-
-        for n in range(3):
-            @pl.when(kids_of[n])
-            def _():
-                remote(whole, whole, s_down.at[kind, n], r_fin.at[kind, 0], peers[n]).wait_send()
+        for here, whole in ((first, whole_first), (last, whole_last)):
+            @pl.when(here & jnp.logical_not(root_of))
+            def _():
+                remote(whole, whole, s_up.at[kind], r_fin.at[kind, 0], parent_of).wait_send()
+
+            for n in range(3):
+                @pl.when(here & kids_of[n])
+                def _():
+                    remote(whole, whole, s_down.at[kind, n], r_fin.at[kind, 0], peers[n]).wait_send()
 
     @pl.when(jnp.logical_not(root))
     def _():
@@ -754,6 +791,15 @@
             remote(SR.at[4], SR.at[4], t_down.at[n], q_fin, peers[n]).wait_send()
 
     send_small().wait_send()
+
+    @pl.when(first)
+    def _():
+        lend().wait_send()
+
+    @pl.when(last)
+    def _():
+        give_back().wait_send()
+
 
     for o in range(12):
         store(jnp.int32(o), True)
@@ -785,7 +831,7 @@
     any_spec = pl.BlockSpec(memory_space=pl.ANY)
     vmem_spec = pl.BlockSpec(memory_space=pltpu.VMEM)
     line = lax.axis_size("dp") // 2
-    steps = 6 * D // STEP_ROWS
+    steps = 13 * (D // 2) // STEP_ROWS
     return pl.pallas_call(
         partial(layer_kernel, line),
         name="layers",
@@ -811,7 +857,7 @@
             pltpu.VMEM((half, D), F32),
             pltpu.VMEM((4 * half, D), BF),
             pltpu.VMEM((2, 2 * half, D), BF),
-            pltpu.VMEM((12, D // 2, D), BF),
+            pltpu.VMEM((13, D // 2, D), BF),
             pltpu.VMEM((2, D // 2, D), BF),
             pltpu.VMEM((2, 8, D), F32),
             pltpu.VMEM((8, D), F32),
@@ -822,6 +868,7 @@
             dma((2,)), dma((2,)), dma((12,)), dma((12,)), dma, dma,
             dma, dma, dma((CLASSES,)), dma((CLASSES, 3)), dma((CLASSES, 3, steps)), dma((CLASSES, steps)),
             dma, dma((3,)), dma((3,)), dma, pltpu.SemaphoreType.REGULAR, pltpu.SemaphoreType.REGULAR,
+            dma, dma, dma, dma,
         ],
         compiler_params=pltpu.CompilerParams(
             collective_id=0, has_side_effects=True, vmem_limit_bytes=64 * MIB

time: 281 us -> 275 us (0.979)
  Pallas kernels: 277 us -> 271 us
    pallas_call x1, Pallas kernels: 265 us -> 260 us  [run_layers(): pl.pallas_call(partial(layer_kernel, line), name='layers', out_shape=(jax...]
where the time goes in v6:
time: 275 us; the launch traced here: 272 us
  Pallas kernels  271 us (99%)
    pallas_call x1, Pallas kernels, run_layers(): pl.pallas_call(partial(layer_kernel, line), name='layers', out_shape=(jax...  260 us
    pallas_call x1, Pallas kernels, results(): pl.pallas_call(result_kernel, name='results', grid=(RESULT_STEPS,), out_s...  11.9 us

profile of v6, /device:TPU:4, one launch (start us, length us, event | category | flops | bytes accessed | tf_op | source)
XLA Modules:
  0.0 272.3 jit_solution(6610241216434964115)
XLA Ops:
  0.6 259.6 %layers.1 = (bf16[3,512,768]{2,1,0:T(8,128)(2,1)}, bf16[3,512,768]{2,1,0:T(8,128)(2,1)}, bf16[768,3072]{1,0:T(8,128)(2,1)}, bf16[1536,768]{1,0:T(8,128)(2,1)}, f32[8,768]{1,0:T(8,128)}) custom-call(bf16[3,512,768]{2,1,0:T(8,128)(2,1)} %tok.1, bf16[3,512,768]{2,1,0:T(8,128)(2,1)} %cot.1, s32[3]{0:T(128)} %lens.1, bf16[768,3072]{1,0:T(8,128)(2,1)} %bitcast.11, ...), custom_call_target="tpu_custom_call" | custom-call | flops 60000002048 | bytes 40000000 | tf_op jit(solution)/shard_map/layers/pallas_call | solution.py:835
  260.2 11.9 %results.1 = (bf16[1536,768]{1,0:T(8,128)(2,1)}, bf16[1536,768]{1,0:T(8,128)(2,1)}, f32[768,3072]{1,0:T(8,128)}, f32[1536,768]{1,0:T(8,128)}, f32[1,768]{1,0:T(1...) custom-call(bf16[1536,768]{1,0:T(8,128)(2,1)} %bitcast.8, bf16[1536,768]{1,0:T(8,128)(2,1)} %bitcast.9, ...), custom_call_target="tpu_custom_call" | custom-call | tf_op jit(solution)/shard_map/results/pallas_call | solution.py:903

commit v7 on v6

--- a/solution.py
+++ b/solution.py
@@ -17,7 +17,7 @@
 NN = (((1,), (0,)), ((), ()))
 NT = (((1,), (1,)), ((), ()))
 TN = (((0,), (0,)), ((), ()))
-LN_ROWS = 128
+LN_ROWS = 256
 W_ORDER = (1, 2, 0, 3)
 FIRST = (slice(0, 256), slice(256, 768))
 LAST = (slice(0, 512), slice(512, 768))

time: 275 us -> 273 us (level)
  no operation moved by 1% of the time
where the time goes in v7:
time: 273 us; the launch traced here: 270 us
  Pallas kernels  269 us (99%)
    pallas_call x1, Pallas kernels, run_layers(): pl.pallas_call(partial(layer_kernel, line), name='layers', out_shape=(jax...  257 us
    pallas_call x1, Pallas kernels, results(): pl.pallas_call(result_kernel, name='results', grid=(RESULT_STEPS,), out_s...  11.9 us

profile of v7, /device:TPU:4, one launch (start us, length us, event | category | flops | bytes accessed | tf_op | source)
XLA Modules:
  0.0 270.0 jit_solution(2363908991170816692)
XLA Ops:
  0.6 257.3 %layers.1 = (bf16[3,512,768]{2,1,0:T(8,128)(2,1)}, bf16[3,512,768]{2,1,0:T(8,128)(2,1)}, bf16[768,3072]{1,0:T(8,128)(2,1)}, bf16[1536,768]{1,0:T(8,128)(2,1)}, f32[8,768]{1,0:T(8,128)}) custom-call(bf16[3,512,768]{2,1,0:T(8,128)(2,1)} %tok.1, bf16[3,512,768]{2,1,0:T(8,128)(2,1)} %cot.1, s32[3]{0:T(128)} %lens.1, bf16[768,3072]{1,0:T(8,128)(2,1)} %bitcast.11, ...), custom_call_target="tpu_custom_call" | custom-call | flops 60000002048 | bytes 40000000 | tf_op jit(solution)/shard_map/layers/pallas_call | solution.py:835
  257.9 11.9 %results.1 = (bf16[1536,768]{1,0:T(8,128)(2,1)}, bf16[1536,768]{1,0:T(8,128)(2,1)}, f32[768,3072]{1,0:T(8,128)}, f32[1536,768]{1,0:T(8,128)}, f32[1,768]{1,0:T(1...) custom-call(bf16[1536,768]{1,0:T(8,128)(2,1)} %bitcast.8, bf16[1536,768]{1,0:T(8,128)(2,1)} %bitcast.9, ...), custom_call_target="tpu_custom_call" | custom-call | tf_op jit(solution)/shard_map/results/pallas_call | solution.py:903
